TPU v7x, 256 devices: a whole 4x4x8 slice. The times are simulated.
256 devices in a mesh: gx: 16 (over z, y_lo), gy: 4 (over y_hi, core), gz: 4 (over x).
Axes of the slice: x: 4, y: 4 (y_hi: 2, y_lo: 2; y = y_hi * 2 + y_lo), z: 8, core: 2. Of those that a mesh axis runs over, the one named last changes fastest.
Arguments:
- seg_rel: float32 [3, 1048576], P(None, ('gx', 'gy', 'gz')), may hold values from -0.5 to 0.5
- burgers: float32 [3, 1048576], P(None, ('gx', 'gy', 'gz')), may hold values from -5 to 5
- line_vec: float32 [3, 1048576], P(None, ('gx', 'gy', 'gz')), may hold values from -5 to 5
- seg_cell: int32 [1048576], P(('gx', 'gy', 'gz')), may hold values from 0 to 15
- ghost_tiles: int32 [2048], P(('gx', 'gy', 'gz')), may hold values from 0 to 31
- ghost_count: int32 [256], P(('gx', 'gy', 'gz')), may hold values from 1 to 8, as said below
- pair_target: int32 [32768], P(('gx', 'gy', 'gz')), may hold values from 0 to 31
- pair_source: int32 [32768], P(('gx', 'gy', 'gz')), may hold values from 0 to 247, as said below
- pair_group: int32 [32768], P(('gx', 'gy', 'gz')), may hold values from 0 to 1
- pair_count: int32 [256], P(('gx', 'gy', 'gz')), may hold values from 16 to 128, as said below
- node_dest: int32 [2, 1048576], P(None, ('gx', 'gy', 'gz')), may hold values from 0 to 107519, as said below
Outputs:
- new_offset: float32 [3, 1048576], P(None, ('gx', 'gy', 'gz'))
- node_force: float32 [3, 1048576], P(None, ('gx', 'gy', 'gz'))
Inputs may be any that keep to these rules, and one draw needn't show every extreme that they name: Each domain's ghost list is live in its first ghost_count entries; some domain has all 8 live. `pair_count`: some domain has all 128 slots live. `pair_source`: values below 32 name own tiles; 32 + 8 t + g names ghost g of the neighbour in slot t, never t = 13. `node_dest`: A value is t * 4096 + n with direction slot t below 27; when t is not 13, n is below 1024.
All inputs are finite; a program needn't handle non-finite values.
Results may differ from a plain program's by a relative error of at most 0.0003.
Values sent between devices are 32-bit elements; how exact they have to be, the bound alone decides.
A program may use at most 128 MiB of HBM per device.

v0:
```python
import jax
import jax.numpy as jnp
from jax import lax
from jax.sharding import PartitionSpec as P

TILE = 128
COMP = 6
TERMS = 35
CELL_Y = 4
CELL_Z = 4
SWEEPS = 2
CELL_DEV = 16


CORE2 = 0.25
NEAR_SCALE = 0.05
FAR_SCALE = 0.002
STEP_SIZE = 0.1
HIGH = lax.Precision.HIGHEST
exponents = [
    (a, b, degree - a - b)
    for degree in range(5)
    for a in range(degree, -1, -1)
    for b in range(degree - a, -1, -1)
]


def extended(cells, sides, width):
    for axis, dim in sides:
        count = lax.axis_size(axis)
        ends = count - 1
        head = lax.slice_in_dim(cells, 0, width, axis=dim)
        tail = lax.slice_in_dim(cells, cells.shape[dim] - width, cells.shape[dim], axis=dim)
        cells = jnp.concatenate(
            [
                lax.ppermute(tail, axis, [(i, (i + 1) % count) for i in range(ends)]),
                cells,
                lax.ppermute(head, axis, [((i + 1) % count, i) for i in range(ends)]),
            ],
            axis=dim,
        )
    return cells


def monomials(unit):
    return jnp.stack([unit[0] ** a * unit[1] ** b * unit[2] ** c for a, b, c in exponents])


def symmetric_part(burgers, line_vec):
    return jnp.stack(
        [
            burgers[0] * line_vec[0],
            burgers[1] * line_vec[1],
            burgers[2] * line_vec[2],
            0.5 * (burgers[0] * line_vec[1] + burgers[1] * line_vec[0]),
            0.5 * (burgers[1] * line_vec[2] + burgers[2] * line_vec[1]),
            0.5 * (burgers[0] * line_vec[2] + burgers[2] * line_vec[0]),
        ]
    )


def moment_terms(offset, burgers, line_vec):
    table = symmetric_part(burgers, line_vec)[:, None, :] * monomials(2.0 * offset)[None, :, :]
    return table.reshape(COMP * TERMS, offset.shape[-1])


def stress_force(per_segment, offset, burgers, line_vec):
    stress = jnp.sum(per_segment.reshape(COMP, TERMS, -1) * monomials(2.0 * offset)[None], axis=1)
    push_x = stress[0] * burgers[0] + stress[3] * burgers[1] + stress[5] * burgers[2]
    push_y = stress[3] * burgers[0] + stress[1] * burgers[1] + stress[4] * burgers[2]
    push_z = stress[5] * burgers[0] + stress[4] * burgers[1] + stress[2] * burgers[2]
    return jnp.stack(
        [
            push_y * line_vec[2] - push_z * line_vec[1],
            push_z * line_vec[0] - push_x * line_vec[2],
            push_x * line_vec[1] - push_y * line_vec[0],
        ]
    )


def pair_force(targets, sources):
    separation = targets[0:3, :, :, None] - sources[0:3, :, None, :]
    radius2 = jnp.sum(separation * separation, axis=0) + CORE2
    inverse3 = 1.0 / (radius2 * jnp.sqrt(radius2))
    burg_dot = jnp.sum(targets[3:6, :, :, None] * sources[3:6, :, None, :], axis=0)
    line_dot = jnp.sum(targets[6:9, :, :, None] * sources[6:9, :, None, :], axis=0)
    weight = burg_dot * line_dot * inverse3
    return jnp.sum(weight[None] * separation, axis=-1)


def cell_coords(along_x, along_y, along_z, local):
    return jnp.stack(
        [along_x + 0 * local, along_y * CELL_Y + local // CELL_Z, along_z * CELL_Z + local % CELL_Z]
    ).astype(jnp.float32)


def cell_kernel(own_coords, count, size_y, size_z):
    source_ids = jnp.arange(count, dtype=jnp.int32)
    source_dev = source_ids // CELL_DEV
    source_coords = cell_coords(
        source_dev // (size_y * size_z),
        source_dev // size_z % size_y,
        source_dev % size_z,
        source_ids % CELL_DEV,
    )
    distance2 = jnp.zeros((own_coords.shape[1], count), jnp.float32)
    for axis_id in range(3):
        spacing = own_coords[axis_id][:, None] - source_coords[axis_id][None, :]
        distance2 = distance2 + spacing * spacing
    return jnp.where(distance2 > 3.5, 1.0 / jnp.sqrt(jnp.maximum(distance2, 1.0)), 0.0)


def near_forces(buffer, target_ids, source_ids, active, live_pairs, tiles_dev):
    block_pairs = 16
    tile_ids = jnp.arange(tiles_dev, dtype=jnp.int32)

    def advance(block_id, running):
        begin_at = block_id * block_pairs
        target_block = lax.dynamic_slice_in_dim(target_ids, begin_at, block_pairs)
        source_block = lax.dynamic_slice_in_dim(source_ids, begin_at, block_pairs)
        active_block = lax.dynamic_slice_in_dim(active, begin_at, block_pairs)
        slot_ids = begin_at + jnp.arange(block_pairs, dtype=jnp.int32)
        weights = active_block * (slot_ids < live_pairs).astype(jnp.float32)
        contrib = pair_force(buffer[:, target_block], buffer[:, source_block])
        select = (target_block[:, None] == tile_ids[None, :]).astype(jnp.float32) * weights[:, None]
        return running + jnp.einsum("pn,cpi->cni", select, contrib, precision=HIGH)

    blocks_used = (live_pairs + block_pairs - 1) // block_pairs
    result = lax.fori_loop(0, blocks_used, advance, jnp.zeros((3, tiles_dev, TILE), jnp.float32))
    return result.reshape(3, tiles_dev * TILE)


def on_device(
    seg_rel,
    burgers,
    line_vec,
    seg_cell,
    ghost_tiles,
    ghost_count,
    pair_target,
    pair_source,
    pair_group,
    pair_count,
    node_dest,
):
    size_x = lax.axis_size("gx")
    size_y = lax.axis_size("gy")
    size_z = lax.axis_size("gz")
    along_x = lax.axis_index("gx")
    along_y = lax.axis_index("gy")
    along_z = lax.axis_index("gz")
    device = (along_x * size_y + along_y) * size_z + along_z
    domains = size_x * size_y * size_z
    segments = seg_rel.shape[1]
    tiles_dev = segments // TILE
    ghosts = ghost_tiles.shape[0]
    boundary = segments // 4
    local_ids = jnp.arange(CELL_DEV, dtype=jnp.int32)
    own_coords = cell_coords(along_x, along_y, along_z, local_ids)
    onehot = (local_ids[:, None] == seg_cell[None, :]).astype(jnp.float32)
    anchors = jnp.dot(own_coords, onehot, precision=HIGH)
    moments = jnp.dot(moment_terms(seg_rel, burgers, line_vec), onehot.T, precision=HIGH)
    grid = lax.dynamic_update_slice(
        jnp.zeros((COMP * TERMS, domains * CELL_DEV), jnp.float32),
        moments,
        (jnp.zeros((), jnp.int32), device * CELL_DEV),
    )
    grid = lax.psum(grid, ("gx", "gy", "gz"))
    kernel = cell_kernel(own_coords, domains * CELL_DEV, size_y, size_z)
    expansion = jnp.dot(grid, kernel.T, precision=HIGH)
    live_ghost = (jnp.arange(ghosts, dtype=jnp.int32) < ghost_count[0]).astype(jnp.float32)
    dest_flat = node_dest.reshape(-1)
    direction = dest_flat // segments
    slot_ids = dest_flat % segments
    centre_ids = jnp.where(direction == 13, slot_ids, segments)
    leaving_ids = jnp.where(direction == 13, 27 * boundary, direction * boundary + slot_ids)
    offset_now = seg_rel
    node_total = jnp.zeros((3, segments), jnp.float32)
    for sweep in range(SWEEPS):
        positions = anchors + 0.5 + offset_now
        own_tiles = jnp.concatenate([positions, burgers, line_vec], axis=0).reshape(
            9, tiles_dev, TILE
        )
        payload = (own_tiles[:, ghost_tiles] * live_ghost[None, :, None])[None, None, None]
        beside_all = extended(payload, (("gx", 0), ("gy", 1), ("gz", 2)), 1)
        neighbours = beside_all.transpose(3, 0, 1, 2, 4, 5).reshape(9, 27 * ghosts, TILE)
        buffer = jnp.concatenate([own_tiles, neighbours], axis=1)
        active = (pair_group == sweep).astype(jnp.float32)
        near = near_forces(buffer, pair_target, pair_source, active, pair_count[0], tiles_dev)
        per_segment = jnp.dot(expansion, onehot, precision=HIGH)
        far = stress_force(per_segment, offset_now, burgers, line_vec)
        forces = FAR_SCALE * far + NEAR_SCALE * near
        offset_now = offset_now + STEP_SIZE * forces
        halves = 0.5 * forces
        values = jnp.concatenate([halves, halves], axis=1).T
        centre = jax.ops.segment_sum(values, centre_ids, segments + 1)[:segments].T
        leaving = jax.ops.segment_sum(values, leaving_ids, 27 * boundary + 1)[: 27 * boundary]
        leaving = leaving.reshape(3, 3, 3, boundary, 3).transpose(0, 1, 2, 4, 3)
        gathered = extended(leaving, (("gx", 0), ("gy", 1), ("gz", 2)), 1)
        received = jnp.zeros((3, boundary), jnp.float32)
        for pick_x in (0, 2, 4):
            for pick_y in (0, 2, 4):
                for pick_z in (0, 2, 4):
                    if (pick_x, pick_y, pick_z) != (2, 2, 2):
                        received = received + gathered[pick_x, pick_y, pick_z]
        node_total = node_total + centre + jnp.pad(received, ((0, 0), (0, segments - boundary)))
    return (offset_now, node_total)


def solution(mesh):
    return jax.shard_map(
        on_device,
        mesh=mesh,
        in_specs=(
            P(None, ("gx", "gy", "gz")),
            P(None, ("gx", "gy", "gz")),
            P(None, ("gx", "gy", "gz")),
            P(("gx", "gy", "gz")),
            P(("gx", "gy", "gz")),
            P(("gx", "gy", "gz")),
            P(("gx", "gy", "gz")),
            P(("gx", "gy", "gz")),
            P(("gx", "gy", "gz")),
            P(("gx", "gy", "gz")),
            P(None, ("gx", "gy", "gz")),
        ),
        out_specs=(P(None, ("gx", "gy", "gz")), P(None, ("gx", "gy", "gz"))),
        check_vma=False,
    )
```

profile of v0, /device:TPU:35, one launch (start us, length us, event | category | flops | bytes accessed | tf_op | source)
XLA Modules:
  0.0 804.8 jit_solution(9263327919960228062)
XLA Ops:
  13.4 2.7 collective-permute-start.1
  35.0 3.1 collective-permute-start.3
  38.2 4.7 collective-permute-start.2
  48.7 3.1 collective-permute-start.4
  53.1 3.2 collective-permute-done.5
  60.0 55.8 %while.22 = (s32[]{:T(128)}, f32[3,32,128]{2,1,0:T(8,128)S(1)}, s32[]{:T(128)}, s32[128]{0:T(128)S(1)}, f32[9,248,128]{2,0,1:T(8,128)S(1)}, /*index=5*/s32[128]{...) while((s32[]{:T(128)}, f32[3,32,128]{2,1,0:T(8,128)S(1)}, ...), condition=%wide.region_7.8_spmd.clone, body=%wide.region_2.7_spmd.clone.sunk | while | flops 10757270 | bytes 9626619 | solution.py:129
  116.4 186.3 %all-reduce.4.cloned.1.call-done = f32[210,4096]{0,1:T(8,128)} async-done(((f32[210,4096]{0,1:T(8,128)}), f32[210,4096]{0,1:T(8,128)}) %all-reduce.4.cloned.1.call-update) | async-done | bytes 3440656 | tf_op jit(solution)/shard_map/psum | solution.py:168
  302.7 4.4 fusion.37
  311.0 3.0 multiply_reduce_fusion.5
  316.1 2.8 collective-permute-start.7
  322.6 2.7 multiply_reduce_fusion.4
  328.3 51.7 %scatter_custom_fusion.1 = f32[27649,3]{1,0:T(8,128)} fusion(s32[8192]{0:T(1024)} %bitcast.217, f32[8192,3]{1,0:T(8,128)} %copy.168, f32[]{:T(128)} %constant.196.clone.1), kind=kCustom, calls=%fused_computation.60 | custom fusion | flops 24576 | bytes 332300 | tf_op jit(solution)/shard_map/scatter-add | solution.py:197
  379.9 10.1 %slice.707 = f32[27648,3]{1,0:T(8,128)} slice(f32[27649,3]{1,0:T(8,128)} %scatter_custom_fusion.1), slice={[0:27648], [0:3]} | slice | bytes 663552 | tf_op jit(solution)/shard_map/slice | solution.py:197
  390.0 9.0 %copy.170 = f32[3,3,3,1024,3]{3,0,4,2,1:T(4,128)S(1)} copy(f32[3,3,3,1024,3]{4,3,2,1,0:T(8,128)} %bitcast.192) | data formatting | bytes 663552 | tf_op jit(solution)/shard_map/reshape | solution.py:198
  399.2 3.7 collective-permute-start.13
  405.6 4.6 collective-permute-start.9
  410.2 4.4 collective-permute-start.8
  418.5 5.1 collective-permute-start.14
  423.7 44.8 %scatter_custom_fusion = f32[4097,3]{1,0:T(8,128)S(1)} fusion(s32[8192]{0:T(1024)} %bitcast.214, f32[8192,3]{1,0:T(8,128)} %copy.168, f32[]{:T(128)} %constant.196.clone.1), kind=kCustom, calls=%fused_computation.78 | custom fusion | flops 24576 | bytes 49676 | tf_op jit(solution)/shard_map/scatter-add | solution.py:196
  476.4 2.7 collective-permute-start.10
  483.0 3.3 collective-permute-start.17
  496.7 77.9 %while.23 = (s32[]{:T(128)}, f32[3,32,128]{2,1,0:T(8,128)S(1)}, s32[]{:T(128)}, s32[128]{0:T(128)S(1)}, f32[9,248,128]{2,0,1:T(8,128)}, /*index=5*/s32[128]{0:T(...) while((s32[]{:T(128)}, f32[3,32,128]{2,1,0:T(8,128)S(1)}, ...), condition=%wide.region_14.15_spmd.clone, body=%wide.region_9.14_spmd.clone.sunk | while | flops 10757270 | bytes 9626619 | solution.py:129
  578.1 51.5 %scatter_custom_fusion.3 = f32[27649,3]{1,0:T(8,128)} fusion(s32[8192]{0:T(1024)} %bitcast.218, f32[8192,3]{1,0:T(8,128)} %copy.203, f32[]{:T(128)} %constant.196.clone.1), kind=kCustom, calls=%fused_computation.58 | custom fusion | flops 24576 | bytes 332300 | tf_op jit(solution)/shard_map/scatter-add | solution.py:197
  629.5 10.1 %slice.737 = f32[27648,3]{1,0:T(8,128)} slice(f32[27649,3]{1,0:T(8,128)} %scatter_custom_fusion.3), slice={[0:27648], [0:3]} | slice | bytes 663552 | tf_op jit(solution)/shard_map/slice | solution.py:197
  639.6 9.0 %copy.205 = f32[3,3,3,1024,3]{3,0,4,2,1:T(4,128)S(1)} copy(f32[3,3,3,1024,3]{4,3,2,1,0:T(8,128)} %bitcast.193) | data formatting | bytes 663552 | tf_op jit(solution)/shard_map/reshape | solution.py:198
  650.7 3.4 collective-permute-start.18
  660.0 45.7 %scatter_custom_fusion.2 = f32[4097,3]{1,0:T(8,128)} fusion(s32[8192]{0:T(1024)} %bitcast.215, f32[8192,3]{1,0:T(8,128)} %copy.203, f32[]{:T(128)} %constant.196.clone.1), kind=kCustom, calls=%fused_computation.76 | custom fusion | flops 24576 | bytes 49676 | tf_op jit(solution)/shard_map/scatter-add | solution.py:196
  709.7 14.2 %collective-permute-start.20 = (f32[5,1,3,3,1024]{4,1,3,2,0:T(1,128)}, f32[5,1,3,3,1024]{4,1,3,2,0:T(1,128)}, u32[]{:S(2)}, u32[]{:S(2)}) collective-permute-start(f32[5,1,3,3,1024]{4,1,3,2,0:T(1,128)} %copy.206), channel_id=1, source_target_pairs={{0,4},{4,8},{8,12},{1,5},{5,9},{9,13},{2,6},{6,10},{10,14},{3,7},{... | collective-permute-start | bytes 552968 | tf_op jit(solution)/shard_map/ppermute | solution.py:36
  746.5 5.5 bitcast_add_fusion.9
  755.9 3.4 collective-permute-start.22
  787.5 5.6 bitcast_add_fusion
  794.9 2.8 copy.238
  (551 shorter events, 278.7 us)
Async XLA Ops:
  7.2 295.5 %all-reduce.4.cloned.1.call-start = ((), (), s32[]{:S(2)}) async-start(), calls=%async_computation | async-start | bytes 8388608 | tf_op jit(solution)/shard_map/psum | solution.py:168
  13.4 20.6 %collective-permute-start.1 = (f32[1,1,1,9,8,128]{5,3,4,2,1,0:T(8,128)}, f32[1,1,1,9,8,128]{5,3,4,2,1,0:T(8,128)}, u32[]{:S(2)}, u32[]{:S(2)}) collective-permute-start(f32[1,1,1,9,8,128]{5,3,4,2,1,0:T(8,128)} %bitcast_multiply_fusion.1), channel_id=1, source_target_pairs={{16,0},{32,16},{48,32},{64,48},{80,64},{96,80},{112,96},{128,112},... | collective-permute-start | bytes 110600 | tf_op jit(solution)/shard_map/ppermute | solution.py:38
  16.2 17.9 %collective-permute-start = (f32[1,1,1,9,8,128]{5,3,4,2,1,0:T(8,128)}, f32[1,1,1,9,8,128]{5,3,4,2,1,0:T(8,128)}, u32[]{:S(2)}, u32[]{:S(2)}) collective-permute-start(f32[1,1,1,9,8,128]{5,3,4,2,1,0:T(8,128)} %bitcast_multiply_fusion.1), channel_id=1, source_target_pairs={{0,16},{16,32},{32,48},{48,64},{64,80},{80,96},{96,112},{112,128},... | collective-permute-start | bytes 110600 | tf_op jit(solution)/shard_map/ppermute | solution.py:36
  31.6 11.3 %copy-start.29 = (s32[1,16]{1,0:T(1,128)S(1)}, s32[1,16]{1,0:T(1,128)}, u32[]{:S(2)}) copy-start(s32[1,16]{1,0:T(1,128)} %copy-done.28) | copy-start | bytes 196
  31.6 11.3 %copy-start.31 = (s32[1,16]{1,0:T(1,128)S(1)}, s32[1,16]{1,0:T(1,128)}, u32[]{:S(2)}) copy-start(s32[1,16]{1,0:T(1,128)} %copy-done.30) | copy-start | bytes 196
  31.6 11.3 %copy-start.35 = (s32[3]{0:T(128)S(1)}, s32[3]{0:T(128)}, u32[]{:S(2)}) copy-start(s32[3]{0:T(128)} %copy-done.34) | copy-start | bytes 40
  31.6 20.2 %copy-start.36 = (s32[128]{0:T(128)S(1)}, s32[128]{0:T(128)}, u32[]{:S(2)}) copy-start(s32[128]{0:T(128)} %param.23) | copy-start | bytes 1540
  35.0 9.3 %collective-permute-start.3 = (f32[3,1,1,9,8,128]{5,3,4,2,1,0:T(8,128)S(1)}, f32[3,1,1,9,8,128]{5,3,4,2,1,0:T(8,128)S(1)}, u32[]{:S(2)}, u32[]{:S(2)}) collective-permute-start(f32[3,1,1,9,8,128]{5,3,4,2,1,0:T(8,128)S(1)} %pad_maximum_fusion.25), channel_id=1, source_target_pairs={{4,0},{8,4},{12,8},{5,1},{9,5},{13,9},{6,2},{10,6},{14,10},{7,3},{... | collective-permute-start | bytes 331784 | tf_op jit(solution)/shard_map/ppermute | solution.py:38
  38.2 7.3 collective-permute-start.2
  46.6 9.8 %collective-permute-start.5 = (f32[3,3,1,9,8,128]{5,4,3,2,1,0:T(8,128)S(1)}, f32[3,3,1,9,8,128]{5,4,3,2,1,0:T(8,128)S(1)}, u32[]{:S(2)}, u32[]{:S(2)}) collective-permute-start(f32[3,3,1,9,8,128]{5,4,3,2,1,0:T(8,128)S(1)} %copy.156), channel_id=1, source_target_pairs={{1,0},{2,1},{3,2},{5,4},{6,5},{7,6},{9,8},{10,9},{11,10},{13,12},{... | collective-permute-start | bytes 995336 | tf_op jit(solution)/shard_map/ppermute | solution.py:38
  48.7 9.0 %collective-permute-start.4 = (f32[3,3,1,9,8,128]{5,4,3,2,1,0:T(8,128)S(1)}, f32[3,3,1,9,8,128]{5,4,3,2,1,0:T(8,128)S(1)}, u32[]{:S(2)}, u32[]{:S(2)}) collective-permute-start(f32[3,3,1,9,8,128]{5,4,3,2,1,0:T(8,128)S(1)} %copy.156), channel_id=1, source_target_pairs={{0,1},{1,2},{2,3},{4,5},{5,6},{6,7},{8,9},{9,10},{10,11},{12,13},{... | collective-permute-start | bytes 995336 | tf_op jit(solution)/shard_map/ppermute | solution.py:36
  316.1 88.8 %collective-permute-start.7 = (f32[1,1,1,9,8,128]{5,3,4,2,1,0:T(8,128)S(1)}, f32[1,1,1,9,8,128]{5,3,4,2,1,0:T(8,128)S(1)}, u32[]{:S(2)}, u32[]{:S(2)}) collective-permute-start(f32[1,1,1,9,8,128]{5,3,4,2,1,0:T(8,128)S(1)} %bitcast_multiply_fusion), channel_id=1, source_target_pairs={{16,0},{32,16},{48,32},{64,48},{80,64},{96,80},{112,96},{128,112},... | collective-permute-start | bytes 110600 | tf_op jit(solution)/shard_map/ppermute | solution.py:38
  318.9 86.0 %collective-permute-start.6 = (f32[1,1,1,9,8,128]{5,3,4,2,1,0:T(8,128)S(1)}, f32[1,1,1,9,8,128]{5,3,4,2,1,0:T(8,128)S(1)}, u32[]{:S(2)}, u32[]{:S(2)}) collective-permute-start(f32[1,1,1,9,8,128]{5,3,4,2,1,0:T(8,128)S(1)} %bitcast_multiply_fusion), channel_id=1, source_target_pairs={{0,16},{16,32},{32,48},{48,64},{64,80},{80,96},{96,112},{112,128},... | collective-permute-start | bytes 110600 | tf_op jit(solution)/shard_map/ppermute | solution.py:36
  399.2 15.4 %collective-permute-start.13 = (f32[1,3,3,3,1024]{4,0,3,2,1:T(1,128)S(1)}, f32[1,3,3,3,1024]{4,0,3,2,1:T(1,128)S(1)}, u32[]{:S(2)}, u32[]{:S(2)}) collective-permute-start(f32[1,3,3,3,1024]{4,0,3,2,1:T(1,128)S(1)} %get-tuple-element.264), channel_id=1, source_target_pairs={{16,0},{32,16},{48,32},{64,48},{80,64},{96,80},{112,96},{128,112},... | collective-permute-start | bytes 331784 | tf_op jit(solution)/shard_map/ppermute | solution.py:38
  402.9 11.7 %collective-permute-start.12 = (f32[1,3,3,3,1024]{4,0,3,2,1:T(1,128)S(1)}, f32[1,3,3,3,1024]{4,0,3,2,1:T(1,128)S(1)}, u32[]{:S(2)}, u32[]{:S(2)}) collective-permute-start(f32[1,3,3,3,1024]{4,0,3,2,1:T(1,128)S(1)} %get-tuple-element.263), channel_id=1, source_target_pairs={{0,16},{16,32},{32,48},{48,64},{64,80},{80,96},{96,112},{112,128},... | collective-permute-start | bytes 331784 | tf_op jit(solution)/shard_map/ppermute | solution.py:36
  405.6 66.4 %collective-permute-start.9 = (f32[3,1,1,9,8,128]{5,3,4,2,1,0:T(8,128)}, f32[3,1,1,9,8,128]{5,3,4,2,1,0:T(8,128)S(1)}, u32[]{:S(2)}, u32[]{:S(2)}) collective-permute-start(f32[3,1,1,9,8,128]{5,3,4,2,1,0:T(8,128)} %pad_maximum_fusion.26), channel_id=1, source_target_pairs={{4,0},{8,4},{12,8},{5,1},{9,5},{13,9},{6,2},{10,6},{14,10},{7,3},{... | collective-permute-start | bytes 331784 | tf_op jit(solution)/shard_map/ppermute | solution.py:38
  410.2 61.8 %collective-permute-start.8 = (f32[3,1,1,9,8,128]{5,3,4,2,1,0:T(8,128)}, f32[3,1,1,9,8,128]{5,3,4,2,1,0:T(8,128)}, u32[]{:S(2)}, u32[]{:S(2)}) collective-permute-start(f32[3,1,1,9,8,128]{5,3,4,2,1,0:T(8,128)} %pad_maximum_fusion.26), channel_id=1, source_target_pairs={{0,4},{4,8},{8,12},{1,5},{5,9},{9,13},{2,6},{6,10},{10,14},{3,7},{... | collective-permute-start | bytes 331784 | tf_op jit(solution)/shard_map/ppermute | solution.py:36
  415.7 63.5 %collective-permute-start.15 = (f32[5,1,3,3,1024]{4,1,3,2,0:T(1,128)}, f32[5,1,3,3,1024]{4,1,3,2,0:T(1,128)}, u32[]{:S(2)}, u32[]{:S(2)}) collective-permute-start(f32[5,1,3,3,1024]{4,1,3,2,0:T(1,128)} %copy.172), channel_id=1, source_target_pairs={{4,0},{8,4},{12,8},{5,1},{9,5},{13,9},{6,2},{10,6},{14,10},{7,3},{... | collective-permute-start | bytes 552968 | tf_op jit(solution)/shard_map/ppermute | solution.py:38
  418.5 61.7 %collective-permute-start.14 = (f32[5,1,3,3,1024]{4,1,3,2,0:T(1,128)}, f32[5,1,3,3,1024]{4,1,3,2,0:T(1,128)S(1)}, u32[]{:S(2)}, u32[]{:S(2)}) collective-permute-start(f32[5,1,3,3,1024]{4,1,3,2,0:T(1,128)} %copy.171), channel_id=1, source_target_pairs={{0,4},{4,8},{8,12},{1,5},{5,9},{9,13},{2,6},{6,10},{10,14},{3,7},{... | collective-permute-start | bytes 552968 | tf_op jit(solution)/shard_map/ppermute | solution.py:36
  473.9 18.0 %collective-permute-start.11 = (f32[3,3,1,9,8,128]{5,4,3,2,1,0:T(8,128)}, f32[3,3,1,9,8,128]{5,4,3,2,1,0:T(8,128)}, u32[]{:S(2)}, u32[]{:S(2)}) collective-permute-start(f32[3,3,1,9,8,128]{5,4,3,2,1,0:T(8,128)} %copy.163), channel_id=1, source_target_pairs={{1,0},{2,1},{3,2},{5,4},{6,5},{7,6},{9,8},{10,9},{11,10},{13,12},{... | collective-permute-start | bytes 995336 | tf_op jit(solution)/shard_map/ppermute | solution.py:38
  476.4 16.6 %collective-permute-start.10 = (f32[3,3,1,9,8,128]{5,4,3,2,1,0:T(8,128)}, f32[3,3,1,9,8,128]{5,4,3,2,1,0:T(8,128)}, u32[]{:S(2)}, u32[]{:S(2)}) collective-permute-start(f32[3,3,1,9,8,128]{5,4,3,2,1,0:T(8,128)} %copy.163), channel_id=1, source_target_pairs={{0,1},{1,2},{2,3},{4,5},{5,6},{6,7},{8,9},{9,10},{10,11},{12,13},{... | collective-permute-start | bytes 995336 | tf_op jit(solution)/shard_map/ppermute | solution.py:36
  482.0 12.1 %copy-start.7 = (f32[3,1,1,9,8,128]{5,3,4,2,1,0:T(8,128)S(1)}, f32[3,1,1,9,8,128]{5,3,4,2,1,0:T(8,128)}, u32[]{:S(2)}) copy-start(f32[3,1,1,9,8,128]{5,3,4,2,1,0:T(8,128)} %copy-done.6) | copy-start | bytes 331780
  483.0 242.9 %collective-permute-start.17 = (f32[5,5,1,3,1024]{4,2,3,1,0:T(1,128)}, f32[5,5,1,3,1024]{4,2,3,1,0:T(1,128)}, u32[]{:S(2)}, u32[]{:S(2)}) collective-permute-start(f32[5,5,1,3,1024]{4,2,3,1,0:T(1,128)} %copy.178), channel_id=1, source_target_pairs={{1,0},{2,1},{3,2},{5,4},{6,5},{7,6},{9,8},{10,9},{11,10},{13,12},{... | collective-permute-start | bytes 921608 | tf_op jit(solution)/shard_map/ppermute | solution.py:38
  489.7 238.1 %collective-permute-start.16 = (f32[5,5,1,3,1024]{4,2,3,1,0:T(1,128)}, f32[5,5,1,3,1024]{4,2,3,1,0:T(1,128)}, u32[]{:S(2)}, u32[]{:S(2)}) collective-permute-start(f32[5,5,1,3,1024]{4,2,3,1,0:T(1,128)} %copy.175), channel_id=1, source_target_pairs={{0,1},{1,2},{2,3},{4,5},{5,6},{6,7},{8,9},{9,10},{10,11},{12,13},{... | collective-permute-start | bytes 921608 | tf_op jit(solution)/shard_map/ppermute | solution.py:36
  496.7 77.9 %copy-start.9 = (f32[3,4096]{1,0:T(4,128)S(1)}, f32[3,4096]{1,0:T(4,128)}, u32[]{:S(2)}) copy-start(f32[3,4096]{1,0:T(4,128)} %copy-done.8) | copy-start | bytes 147460
  639.6 16.3 %copy-start.24 = (f32[1,1,1,3,1024]{4,1,3,2,0:T(1,128)S(1)}, f32[1,1,1,3,1024]{4,1,3,2,0:T(1,128)}, u32[]{:S(2)}) copy-start(f32[1,1,1,3,1024]{4,1,3,2,0:T(1,128)} %get-tuple-element.307) | copy-start | bytes 36868
  648.8 57.0 %collective-permute-start.19 = (f32[1,3,3,3,1024]{4,0,3,2,1:T(1,128)S(1)}, f32[1,3,3,3,1024]{4,0,3,2,1:T(1,128)S(1)}, u32[]{:S(2)}, u32[]{:S(2)}) collective-permute-start(f32[1,3,3,3,1024]{4,0,3,2,1:T(1,128)S(1)} %get-tuple-element.266), channel_id=1, source_target_pairs={{16,0},{32,16},{48,32},{64,48},{80,64},{96,80},{112,96},{128,112},... | collective-permute-start | bytes 331784 | tf_op jit(solution)/shard_map/ppermute | solution.py:38
  650.7 55.0 %collective-permute-start.18 = (f32[1,3,3,3,1024]{4,0,3,2,1:T(1,128)S(1)}, f32[1,3,3,3,1024]{4,0,3,2,1:T(1,128)S(1)}, u32[]{:S(2)}, u32[]{:S(2)}) collective-permute-start(f32[1,3,3,3,1024]{4,0,3,2,1:T(1,128)S(1)} %get-tuple-element.265), channel_id=1, source_target_pairs={{0,16},{16,32},{32,48},{48,64},{64,80},{80,96},{96,112},{112,128},... | collective-permute-start | bytes 331784 | tf_op jit(solution)/shard_map/ppermute | solution.py:36
  706.9 45.1 %collective-permute-start.21 = (f32[5,1,3,3,1024]{4,1,3,2,0:T(1,128)}, f32[5,1,3,3,1024]{4,1,3,2,0:T(1,128)S(1)}, u32[]{:S(2)}, u32[]{:S(2)}) collective-permute-start(f32[5,1,3,3,1024]{4,1,3,2,0:T(1,128)} %copy.207), channel_id=1, source_target_pairs={{4,0},{8,4},{12,8},{5,1},{9,5},{13,9},{6,2},{10,6},{14,10},{7,3},{... | collective-permute-start | bytes 552968 | tf_op jit(solution)/shard_map/ppermute | solution.py:38
  709.7 42.4 %collective-permute-start.20 = (f32[5,1,3,3,1024]{4,1,3,2,0:T(1,128)}, f32[5,1,3,3,1024]{4,1,3,2,0:T(1,128)}, u32[]{:S(2)}, u32[]{:S(2)}) collective-permute-start(f32[5,1,3,3,1024]{4,1,3,2,0:T(1,128)} %copy.206), channel_id=1, source_target_pairs={{0,4},{4,8},{8,12},{1,5},{5,9},{9,13},{2,6},{6,10},{10,14},{3,7},{... | collective-permute-start | bytes 552968 | tf_op jit(solution)/shard_map/ppermute | solution.py:36
  753.6 13.3 %collective-permute-start.23 = (f32[5,5,1,3,1024]{4,2,3,1,0:T(1,128)S(1)}, f32[5,5,1,3,1024]{4,2,3,1,0:T(1,128)}, u32[]{:S(2)}, u32[]{:S(2)}) collective-permute-start(f32[5,5,1,3,1024]{4,2,3,1,0:T(1,128)S(1)} %copy.213), channel_id=1, source_target_pairs={{1,0},{2,1},{3,2},{5,4},{6,5},{7,6},{9,8},{10,9},{11,10},{13,12},{... | collective-permute-start | bytes 921608 | tf_op jit(solution)/shard_map/ppermute | solution.py:38
  755.9 13.0 %collective-permute-start.22 = (f32[5,5,1,3,1024]{4,2,3,1,0:T(1,128)S(1)}, f32[5,5,1,3,1024]{4,2,3,1,0:T(1,128)}, u32[]{:S(2)}, u32[]{:S(2)}) collective-permute-start(f32[5,5,1,3,1024]{4,2,3,1,0:T(1,128)S(1)} %copy.210), channel_id=1, source_target_pairs={{0,1},{1,2},{2,3},{4,5},{5,6},{6,7},{8,9},{9,10},{10,11},{12,13},{... | collective-permute-start | bytes 921608 | tf_op jit(solution)/shard_map/ppermute | solution.py:36
  (30 other events, 105.6 us)
Sparse Core Ops, SparseCore 0:
  31.8 270.8 all-reduce.3
where the time goes:
time: 819 us; the launch traced here: 805 us
  other arithmetic  320 us (39%)
  waiting for transfers between devices  193 us (24%)
  local copies, waits for them, and re-layouts  174 us (21%)
  starting transfers between devices  82.8 us (10%)
  between operations  16.8 us (2%)
  matrix products  14.5 us (2%)
    psum x1, waiting for transfers between devices, on_device(): grid = lax.psum(grid, ('gx', 'gy', 'gz'))  186 us
    scatter-add x2, other arithmetic, on_device(): jax.ops.segment_sum(values, leaving_ids, 27 * boundary + 1)[:27 * boundary]  103 us
    scatter-add x2, other arithmetic, on_device(): centre = jax.ops.segment_sum(values, centre_ids, segments + 1)[:segments].T  90.5 us
    unnamed x131, local copies, waits for them, and re-layouts  61.2 us
    ppermute x12, starting transfers between devices, extended(): lax.ppermute(tail, axis, [(i, (i + 1) % count) for i in range(ends)])  50.2 us
    gather x28, local copies, waits for them, and re-layouts, advance(): contrib = pair_force(buffer[:, target_block], buffer[:, source_block])  37.7 us
    ppermute x12, starting transfers between devices, extended(): lax.ppermute(head, axis, [((i + 1) % count, i) for i in range(ends)])  32.6 us
    reduce_sum x14, other arithmetic, pair_force(): return jnp.sum(weight[None] * separation, axis=-1)  26.9 us
  transfers between devices with their start and end apart: 25, of which 5 were waited for; matrix products, arithmetic and copies ran while one was open for 57% of the time, Pallas kernels for 0%

commit v1 on v0

v1 whole, which is shorter than its diff:
```python
import functools

import jax
import jax.numpy as jnp
from jax import lax
from jax.experimental import pallas as pl
from jax.experimental.pallas import tpu as pltpu
from jax.sharding import PartitionSpec as P

TILE = 128
SEG = 4096
GROUPS = 4
GHOST_DEV = 8
CELL_DEV = 16
COMP = 6
TERMS = 35
LANE_STEP = 42
PAIRS = 128
CORE2 = 0.25
NEAR_SCALE = 0.05
FAR_SCALE = 0.002
STEP_SIZE = 0.1
MESH = pl.DeviceIdType.MESH
F32 = jnp.float32
BF16 = jnp.bfloat16
EXPONENTS = [
    (a, b, degree - a - b)
    for degree in range(5)
    for a in range(degree, -1, -1)
    for b in range(degree - a, -1, -1)
]
NT = (((1,), (1,)), ((), ()))
TN = (((0,), (0,)), ((), ()))


def vmem(count):
    return [pl.BlockSpec(memory_space=pltpu.VMEM)] * count


def smem(count):
    return [pl.BlockSpec(memory_space=pltpu.SMEM)] * count


def halves_of(value):
    high = value.astype(BF16).astype(F32)
    return high, value - high


def powers(unit):
    square = unit * unit
    return [None, unit, square, square * unit, square * square]


def monomial(u, v, w, exps):
    result = None
    for table, power in zip((u, v, w), exps):
        if power:
            result = table[power] if result is None else result * table[power]
    return result


def symmetric(b, t):
    return [
        b[0] * t[0],
        b[1] * t[1],
        b[2] * t[2],
        0.5 * (b[0] * t[1] + b[1] * t[0]),
        0.5 * (b[1] * t[2] + b[2] * t[1]),
        0.5 * (b[0] * t[2] + b[2] * t[0]),
    ]


class Place:
    def __init__(self, sizes):
        self.sizes = sizes
        self.at = tuple(lax.axis_index(name) for name in ("gx", "gy", "gz"))

    def beside(self, slot, sign=1):
        steps = (slot // 9 - 1, slot // 3 % 3 - 1, slot % 3 - 1)
        where = tuple(a + sign * s for a, s in zip(self.at, steps))
        inside = slot != 13
        for at, size in zip(where, self.sizes):
            inside = jnp.logical_and(inside, jnp.logical_and(at >= 0, at < size))
        return where, inside

    def count_beside(self):
        total = 1
        for at, size in zip(self.at, self.sizes):
            total = total * (3 - (at == 0).astype(jnp.int32) - (at == size - 1).astype(jnp.int32))
        return total - 1


def each_slot(body):
    def step(slot, carry):
        body(slot)
        return carry

    lax.fori_loop(0, 27, step, 0)


def greet_neighbours(place, barrier):
    def greet(slot):
        where, inside = place.beside(slot)

        @pl.when(inside)
        def _():
            pl.semaphore_signal(barrier, inc=1, device_id=where, device_id_type=MESH)

    each_slot(greet)


def expand_kernel(
    sizes,
    rel_ref,
    burg_ref,
    line_ref,
    cell_ref,
    ghost_ref,
    live_ref,
    source_ref,
    base_ref,
    table_ref,
    own,
    payload,
    mono,
    symm,
    gathered,
    contrib,
    arrived,
    ghost_send,
    ghost_recv,
    plane_send,
    plane_recv,
    line_send,
    line_recv,
):
    nx, ny, nz = sizes
    plane = ny * nz
    place = Place(sizes)
    gx, gy, gz = place.at
    here = gy * nz + gz

    def plane_peer(step):
        peer = lax.rem(here + step, plane)
        return (gx, peer // nz, lax.rem(peer, nz))

    def line_peer(step):
        return (lax.rem(gx + step, nx), gy, gz)

    barrier = pltpu.get_barrier_semaphore()
    greet_neighbours(place, barrier)

    def greet_plane(step, carry):
        pl.semaphore_signal(barrier, inc=1, device_id=plane_peer(step), device_id_type=MESH)
        return carry

    def greet_line(step, carry):
        pl.semaphore_signal(barrier, inc=1, device_id=line_peer(step), device_id_type=MESH)
        return carry

    lax.fori_loop(1, plane, greet_plane, 0)
    lax.fori_loop(1, nx, greet_line, 0)

    for tile in range(SEG // TILE):
        lanes = pl.ds(tile * TILE, TILE)
        for row in range(3):
            own[tile // 8, row, pl.ds(tile % 8, 1), :] = rel_ref[pl.ds(row, 1), lanes]
            own[tile // 8, 3 + row, pl.ds(tile % 8, 1), :] = burg_ref[pl.ds(row, 1), lanes]
            own[tile // 8, 6 + row, pl.ds(tile % 8, 1), :] = line_ref[pl.ds(row, 1), lanes]
    for group in range(GROUPS):
        rows = slice(8 * group, 8 * group + 8)
        cell = cell_ref[rows, :]
        rel = [own[group, row] for row in range(3)]
        burg = [own[group, 3 + row] for row in range(3)]
        line = [own[group, 6 + row] for row in range(3)]
        corner = (
            jnp.full((8, TILE), gx, jnp.int32),
            gy * 4 + (cell >> 2),
            gz * 4 + (cell & 3),
        )
        for row in range(3):
            base = corner[row].astype(F32) + 0.5
            base_ref[group, row] = base
            own[group, row] = base + rel[row]
        source_ref[group] = own[group]
        for at, value in enumerate(symmetric(burg, line)):
            symm[pl.ds(at * 32 + 8 * group, 8), :] = value
        u, v, w = (powers(2.0 * value) for value in rel)
        for at, exps in enumerate(EXPONENTS):
            value = monomial(u, v, w, exps)
            mono[pl.ds(at * 32 + 8 * group, 8), :] = (
                jnp.ones((8, TILE), F32) if value is None else value
            )
    for at in range(TERMS, 40):
        mono[pl.ds(at * 32, 32), :] = jnp.zeros((32, TILE), F32)
    for ghost in range(GHOST_DEV):
        tile = ghost_ref[ghost]
        live = jnp.where(ghost < live_ref[0], 1.0, 0.0)
        for row in range(9):
            value = own[tile // 8, row, pl.ds(lax.rem(tile, 8), 1), :]
            payload[row, pl.ds(ghost, 1), :] = value * live

    cells = lax.broadcasted_iota(jnp.int32, (CELL_DEV, TILE), 0)
    moments = jnp.zeros((COMP * CELL_DEV, 40), F32)
    for block in range(4):
        lefts, rights = [], []
        for tile in range(8 * block, 8 * block + 8):
            chosen = cells == cell_ref[pl.ds(tile, 1), :]
            left = jnp.concatenate(
                [
                    jnp.where(chosen, symm[pl.ds(at * 32 + tile, 1), :], 0.0)
                    for at in range(COMP)
                ],
                axis=0,
            )
            right = mono[pl.ds(tile, 40, stride=32), :]
            left_high, left_low = halves_of(left)
            right_high, right_low = halves_of(right)
            lefts += [left_high, left_high, left_low]
            rights += [right_high, right_low, right_high]
        moments = moments + lax.dot_general(
            jnp.concatenate(lefts, axis=1).astype(BF16),
            jnp.concatenate(rights, axis=1).astype(BF16),
            NT,
            preferred_element_type=F32,
        )
    wide = jnp.concatenate([moments, jnp.zeros((COMP * CELL_DEV, TILE - 40), F32)], axis=1)
    mine = pl.ds(pl.multiple_of(here * CELL_DEV, CELL_DEV), CELL_DEV)
    for half in range(2):
        total = jnp.zeros((CELL_DEV, TILE), F32)
        for third in range(3):
            at = (3 * half + third) * CELL_DEV
            part = wide[at : at + CELL_DEV]
            total = total + (pltpu.roll(part, third * LANE_STEP, 1) if third else part)
        gathered[mine, pl.ds(half * TILE, TILE)] = total

    pl.semaphore_wait(barrier, place.count_beside() + plane - 1 + nx - 1)

    def plane_copy(step):
        return pltpu.make_async_remote_copy(
            src_ref=gathered.at[mine],
            dst_ref=gathered.at[mine],
            send_sem=plane_send.at[step],
            recv_sem=plane_recv.at[step],
            device_id=plane_peer(step),
            device_id_type=MESH,
        )

    def ghost_copy(slot):
        where, inside = place.beside(slot)
        copy = pltpu.make_async_remote_copy(
            src_ref=payload,
            dst_ref=source_ref.at[GROUPS + 26 - slot],
            send_sem=ghost_send.at[slot],
            recv_sem=ghost_recv.at[26 - slot],
            device_id=where,
            device_id_type=MESH,
        )
        return copy, inside

    def start_plane(step, carry):
        plane_copy(step).start()
        return carry

    lax.fori_loop(1, plane, start_plane, 0)

    def start_ghost(slot):
        copy, inside = ghost_copy(slot)

        @pl.when(inside)
        def _():
            copy.start()

        @pl.when(jnp.logical_not(inside))
        def _():
            source_ref[GROUPS + slot] = jnp.zeros((9, GHOST_DEV, TILE), F32)

    each_slot(start_ghost)

    rows, columns = nx * CELL_DEV, plane * CELL_DEV
    row = lax.broadcasted_iota(jnp.int32, (rows, columns), 0)
    column = lax.broadcasted_iota(jnp.int32, (rows, columns), 1)
    peer = column >> 4
    step_x = (row >> 4) - gx
    step_y = gy * 4 + ((row >> 2) & 3) - (peer // nz * 4 + ((column >> 2) & 3))
    step_z = gz * 4 + (row & 3) - (peer % nz * 4 + (column & 3))
    distance2 = (step_x * step_x + step_y * step_y + step_z * step_z).astype(F32)
    weight = jnp.where(distance2 > 3.5, 1.0 / jnp.sqrt(jnp.maximum(distance2, 1.0)), 0.0)

    def wait_plane(step, carry):
        plane_copy(step).wait()
        return carry

    lax.fori_loop(1, plane, wait_plane, 0)
    contrib[...] = jnp.dot(
        weight, gathered[...], precision=lax.Precision.HIGHEST, preferred_element_type=F32
    )

    def line_copy(step):
        there = lax.rem(gx + step, nx)
        return pltpu.make_async_remote_copy(
            src_ref=contrib.at[pl.ds(pl.multiple_of(there * CELL_DEV, CELL_DEV), CELL_DEV)],
            dst_ref=arrived.at[step],
            send_sem=line_send.at[step],
            recv_sem=line_recv.at[step],
            device_id=line_peer(step),
            device_id_type=MESH,
        )

    def start_line(step, carry):
        line_copy(step).start()
        return carry

    lax.fori_loop(1, nx, start_line, 0)
    total = contrib[pl.ds(pl.multiple_of(gx * CELL_DEV, CELL_DEV), CELL_DEV), :]

    def wait_line(step, carry):
        line_copy(step).wait()
        return carry

    lax.fori_loop(1, nx, wait_line, 0)
    for step in range(1, nx):
        total = total + arrived[step]
    full = jnp.concatenate([total, jnp.zeros((TILE - CELL_DEV, 2 * TILE), F32)], axis=0)
    table_ref[pl.ds(0, TILE), :] = full[:, :TILE].T
    table_ref[pl.ds(TILE, TILE), :] = full[:, TILE:].T
    source_ref[GROUPS + 13] = jnp.zeros((9, GHOST_DEV, TILE), F32)

    def wait_ghost_send(slot):
        copy, inside = ghost_copy(slot)

        @pl.when(inside)
        def _():
            copy.wait_send()

    def wait_ghost_recv(slot):
        copy, _ = ghost_copy(slot)
        _, inside = place.beside(slot, -1)

        @pl.when(inside)
        def _():
            copy.wait_recv()

    each_slot(wait_ghost_send)
    each_slot(wait_ghost_recv)


def far_force(group, offset, burg, line, cell, table_ref):
    u, v, w = (powers(2.0 * value) for value in offset)
    stress = [None] * COMP
    for at, exps in enumerate(EXPONENTS):
        value = monomial(u, v, w, exps)
        for comp in range(COMP):
            row = comp // 3 * TILE + comp % 3 * LANE_STEP + at
            entry = jnp.broadcast_to(table_ref[pl.ds(row, 1), :], (8, TILE))
            term = jnp.take_along_axis(entry, cell, axis=1, mode="promise_in_bounds")
            if value is not None:
                term = term * value
            stress[comp] = term if stress[comp] is None else stress[comp] + term
    push_x = stress[0] * burg[0] + stress[3] * burg[1] + stress[5] * burg[2]
    push_y = stress[3] * burg[0] + stress[1] * burg[1] + stress[4] * burg[2]
    push_z = stress[5] * burg[0] + stress[4] * burg[1] + stress[2] * burg[2]
    return [
        push_y * line[2] - push_z * line[1],
        push_z * line[0] - push_x * line[2],
        push_x * line[1] - push_y * line[0],
    ]


def split_rows(source_ref, group):
    highs, lows = [], []
    for a in range(3):
        for c in range(3):
            high, low = halves_of(source_ref[group, 3 + a] * source_ref[group, 6 + c])
            highs.append(high)
            lows.append(low)
    return highs, lows


def near_pass(
    sweep, count_ref, target_ref, from_ref, group_ref, source_ref, places, sides, targets, near, chosen
):
    zero = jnp.zeros((8, TILE), F32)

    def fill(group, carry):
        highs, lows = split_rows(source_ref, group)
        at = pl.multiple_of(group * 256, 256)
        for row, value in enumerate(highs + highs + lows + [zero] * 5):
            sides[pl.ds(at + 8 * row, 8), :] = value
        return carry

    lax.fori_loop(0, GROUPS + 27, fill, 0)
    for group in range(GROUPS):
        highs, lows = split_rows(source_ref, group)
        for row, value in enumerate(highs + lows + highs + [zero] * 5):
            targets[pl.ds(group * 256 + 8 * row, 8), :] = value
    near[...] = jnp.zeros(near.shape, F32)

    def choose(pair, used):
        chosen[used] = pair
        return used + (group_ref[pair] == sweep).astype(jnp.int32)

    used = lax.fori_loop(0, count_ref[0], choose, 0)

    def one(at, carry):
        pair = chosen[at]
        source = from_ref[pair]
        target = target_ref[pair]
        left = sides[pl.ds((source >> 3) * 256 + (source & 7), 32, stride=8), :]
        right = targets[pl.ds((target >> 3) * 256 + (target & 7), 32, stride=8), :]
        strength = lax.dot_general(
            left.astype(BF16), right.astype(BF16), TN, preferred_element_type=F32
        )
        there = places[pl.ds((source >> 3) * 64 + (source & 7), 8, stride=8), :].T
        spot = (target >> 3) * 64 + (target & 7)
        here = [places[pl.ds(spot + 8 * row, 1), :] for row in range(3)]
        totals = [jnp.zeros((8, TILE), F32)] * 3
        for chunk in range(16):
            span = slice(8 * chunk, 8 * chunk + 8)
            gaps = [here[row] - there[span, row : row + 1] for row in range(3)]
            radius2 = gaps[0] * gaps[0] + gaps[1] * gaps[1] + gaps[2] * gaps[2] + CORE2
            inverse = lax.rsqrt(radius2)
            weight = strength[span, :] * (inverse * inverse * inverse)
            totals = [total + weight * gap for total, gap in zip(totals, gaps)]
        spot = (target >> 3) * 24 + (target & 7)
        for row in range(3):
            at_row = pl.ds(spot + 8 * row, 1)
            near[at_row, :] += jnp.sum(totals[row], axis=0, keepdims=True)
        return carry

    lax.fori_loop(0, used, one, 0)


def forces_of(group, offsets, cell_ref, source_ref, table_ref, near):
    burg = [source_ref[group, 3 + row] for row in range(3)]
    line = [source_ref[group, 6 + row] for row in range(3)]
    cell = cell_ref[pl.ds(8 * group, 8), :]
    far = far_force(group, offsets, burg, line, cell, table_ref)
    return [
        FAR_SCALE * far[row] + NEAR_SCALE * near[pl.ds(group * 24 + 8 * row, 8), :]
        for row in range(3)
    ]


def first_kernel(
    count_ref,
    target_ref,
    from_ref,
    group_ref,
    ghost_ref,
    source_ref,
    base_ref,
    table_ref,
    cell_ref,
    rel_ref,
    offset_ref,
    force_ref,
    places_ref,
    payload_ref,
    places,
    sides,
    targets,
    near,
    chosen,
):
    def spread(group, carry):
        at = pl.multiple_of(group * 64, 64)
        for row in range(3):
            places[pl.ds(at + 8 * row, 8), :] = source_ref[group, row]
        return carry

    lax.fori_loop(0, GROUPS + 27, spread, 0)
    near_pass(
        0, count_ref, target_ref, from_ref, group_ref, source_ref, places, sides, targets, near, chosen
    )
    for tile in range(SEG // TILE):
        for row in range(3):
            offset_ref[tile // 8, row, pl.ds(tile % 8, 1), :] = rel_ref[
                pl.ds(row, 1), pl.ds(tile * TILE, TILE)
            ]
    for group in range(GROUPS):
        offsets = [offset_ref[group, row] for row in range(3)]
        forces = forces_of(group, offsets, cell_ref, source_ref, table_ref, near)
        for row in range(3):
            moved = offsets[row] + STEP_SIZE * forces[row]
            force_ref[group, row] = forces[row]
            offset_ref[group, row] = moved
            places_ref[group, row] = base_ref[group, row] + moved
    for ghost in range(GHOST_DEV):
        tile = ghost_ref[ghost]
        for row in range(3):
            payload_ref[row, pl.ds(ghost, 1), :] = places_ref[tile >> 3, row, pl.ds(tile & 7, 1), :]


def exchange(place, send_of, receive_at, send_sem, recv_sem):
    def copy_of(slot):
        where, inside = place.beside(slot)
        copy = pltpu.make_async_remote_copy(
            src_ref=send_of(slot),
            dst_ref=receive_at(26 - slot),
            send_sem=send_sem.at[slot],
            recv_sem=recv_sem.at[26 - slot],
            device_id=where,
            device_id_type=MESH,
        )
        return copy, inside

    def start(slot):
        copy, inside = copy_of(slot)

        @pl.when(inside)
        def _():
            copy.start()

    def wait(slot):
        copy, inside = copy_of(slot)

        @pl.when(inside)
        def _():
            copy.wait_send()

        arriving, _ = copy_of(26 - slot)

        @pl.when(inside)
        def _():
            arriving.wait_recv()

    return start, wait


def ghosts_kernel(sizes, payload_ref, ghosts_ref, send_sem, recv_sem):
    place = Place(sizes)
    barrier = pltpu.get_barrier_semaphore()
    greet_neighbours(place, barrier)

    def clear(slot):
        _, inside = place.beside(slot)

        @pl.when(jnp.logical_not(inside))
        def _():
            ghosts_ref[slot] = jnp.zeros((3, GHOST_DEV, TILE), F32)

    each_slot(clear)
    pl.semaphore_wait(barrier, place.count_beside())
    start, wait = exchange(
        place, lambda slot: payload_ref, lambda slot: ghosts_ref.at[slot], send_sem, recv_sem
    )
    each_slot(start)
    each_slot(wait)


def second_kernel(
    count_ref,
    target_ref,
    from_ref,
    group_ref,
    source_ref,
    own_ref,
    ghosts_ref,
    table_ref,
    cell_ref,
    offset_ref,
    force_ref,
    dest_ref,
    moved_ref,
    leaving_ref,
    centre_ref,
    places,
    sides,
    targets,
    near,
    values,
    sums,
    chosen,
):
    for group in range(GROUPS):
        for row in range(3):
            places[pl.ds(group * 64 + 8 * row, 8), :] = own_ref[group, row]

    def spread(slot, carry):
        at = pl.multiple_of((GROUPS + slot) * 64, 64)
        for row in range(3):
            places[pl.ds(at + 8 * row, 8), :] = ghosts_ref[slot, row]
        return carry

    lax.fori_loop(0, 27, spread, 0)
    near_pass(
        1, count_ref, target_ref, from_ref, group_ref, source_ref, places, sides, targets, near, chosen
    )
    for group in range(GROUPS):
        offsets = [offset_ref[group, row] for row in range(3)]
        forces = forces_of(group, offsets, cell_ref, source_ref, table_ref, near)
        for row in range(3):
            moved = offsets[row] + STEP_SIZE * forces[row]
            half = 0.5 * (force_ref[group, row] + forces[row])
            for tile in range(8):
                lanes = pl.ds((8 * group + tile) * TILE, TILE)
                moved_ref[pl.ds(row, 1), lanes] = moved[tile : tile + 1]
                values[pl.ds(row, 1), lanes] = half[tile : tile + 1]
    sums[...] = jnp.zeros(sums.shape, F32)
    width = 512
    high_ids = lax.broadcasted_iota(jnp.int32, (128, width), 0)
    low_ids = lax.broadcasted_iota(jnp.int32, (256, width), 0)

    def scatter(block, carry):
        lanes = pl.ds(pl.multiple_of(block * width, width), width)
        parts = [halves_of(values[pl.ds(row, 1), lanes]) for row in range(3)]
        for end in range(2):
            dest = dest_ref[pl.ds(end, 1), lanes]
            node = dest & (SEG - 1)
            slot = dest >> 12
            upper = jnp.where(slot == 13, 0, 16 + 4 * slot) + (node >> 8)
            lower = node & 255
            chosen_rows = high_ids == upper
            left = jnp.concatenate(
                [
                    jnp.where(chosen_rows, parts[row][piece], 0.0).astype(BF16)
                    for row in range(3)
                    for piece in range(2)
                ],
                axis=0,
            )
            right = jnp.where(low_ids == lower, 1.0, 0.0).astype(BF16)
            sums[...] += lax.dot_general(left, right, NT, preferred_element_type=F32)
        return carry

    lax.fori_loop(0, SEG // width, scatter, 0)
    for row in range(3):
        at = 256 * row
        centre_ref[row] = sums[pl.ds(at, 16), :] + sums[pl.ds(at + 128, 16), :]
        for slot in range(27):
            both = sums[pl.ds(at + 16 + 4 * slot, 4), :] + sums[pl.ds(at + 144 + 4 * slot, 4), :]
            leaving_ref[slot, row, pl.ds(0, 4), :] = both[:, :TILE]
            leaving_ref[slot, row, pl.ds(4, 4), :] = both[:, TILE:]


def nodes_kernel(sizes, leaving_ref, centre_ref, out_ref, landed, send_sem, recv_sem):
    place = Place(sizes)
    barrier = pltpu.get_barrier_semaphore()
    greet_neighbours(place, barrier)

    def clear(slot):
        _, inside = place.beside(slot)

        @pl.when(jnp.logical_not(inside))
        def _():
            landed[slot] = jnp.zeros((3, 8, TILE), F32)

    each_slot(clear)
    pl.semaphore_wait(barrier, place.count_beside())
    start, wait = exchange(
        place, lambda slot: leaving_ref.at[slot], lambda slot: landed.at[slot], send_sem, recv_sem
    )
    each_slot(start)
    for row in range(3):
        for part in range(4, 16):
            out_ref[pl.ds(row, 1), pl.ds(256 * part, 256)] = centre_ref[row, pl.ds(part, 1), :]
    each_slot(wait)
    for row in range(3):
        total = landed[0, row]
        for slot in range(1, 27):
            total = total + landed[slot, row]
        for part in range(4):
            for half in range(2):
                lanes = slice(TILE * half, TILE * half + TILE)
                out_ref[pl.ds(row, 1), pl.ds(256 * part + TILE * half, TILE)] = (
                    centre_ref[row, pl.ds(part, 1), lanes]
                    + total[4 * half + part : 4 * half + part + 1]
                )


def on_device(
    sizes,
    seg_rel,
    burgers,
    line_vec,
    seg_cell,
    ghost_tiles,
    ghost_count,
    pair_target,
    pair_source,
    pair_group,
    pair_count,
    node_dest,
):
    nx, ny, nz = sizes
    plane = ny * nz
    cell = seg_cell.reshape(SEG // TILE, TILE)
    shape = jax.ShapeDtypeStruct
    dma = pltpu.SemaphoreType.DMA
    source, base, table = pl.pallas_call(
        functools.partial(expand_kernel, sizes),
        out_shape=(
            shape((GROUPS + 27, 9, 8, TILE), F32),
            shape((GROUPS, 3, 8, TILE), F32),
            shape((2 * TILE, TILE), F32),
        ),
        in_specs=vmem(4) + smem(2),
        out_specs=tuple(vmem(3)),
        scratch_shapes=[
            pltpu.VMEM((GROUPS, 9, 8, TILE), F32),
            pltpu.VMEM((9, GHOST_DEV, TILE), F32),
            pltpu.VMEM((40 * 32, TILE), F32),
            pltpu.VMEM((COMP * 32, TILE), F32),
            pltpu.VMEM((plane * CELL_DEV, 2 * TILE), F32),
            pltpu.VMEM((nx * CELL_DEV, 2 * TILE), F32),
            pltpu.VMEM((nx, CELL_DEV, 2 * TILE), F32),
            dma((27,)),
            dma((27,)),
            dma((plane,)),
            dma((plane,)),
            dma((nx,)),
            dma((nx,)),
        ],
        compiler_params=pltpu.CompilerParams(
            collective_id=0, has_side_effects=True, vmem_limit_bytes=32 << 20
        ),
        name="expand",
    )(seg_rel, burgers, line_vec, cell, ghost_tiles, ghost_count)
    near_scratch = [
        pltpu.VMEM(((GROUPS + 27) * 64, TILE), F32),
        pltpu.VMEM(((GROUPS + 27) * 256, TILE), F32),
        pltpu.VMEM((GROUPS * 256, TILE), F32),
        pltpu.VMEM((GROUPS * 24, TILE), F32),
    ]
    own_shape = shape((GROUPS, 3, 8, TILE), F32)
    offset, force, own, payload = pl.pallas_call(
        first_kernel,
        out_shape=(own_shape, own_shape, own_shape, shape((3, GHOST_DEV, TILE), F32)),
        in_specs=smem(5) + vmem(5),
        out_specs=tuple(vmem(4)),
        scratch_shapes=near_scratch + [pltpu.SMEM((PAIRS,), jnp.int32)],
        compiler_params=pltpu.CompilerParams(vmem_limit_bytes=32 << 20),
        name="first",
    )(
        pair_count,
        pair_target,
        pair_source,
        pair_group,
        ghost_tiles,
        source,
        base,
        table,
        cell,
        seg_rel,
    )
    ghosts = pl.pallas_call(
        functools.partial(ghosts_kernel, sizes),
        out_shape=shape((27, 3, GHOST_DEV, TILE), F32),
        in_specs=vmem(1),
        out_specs=vmem(1)[0],
        scratch_shapes=[dma((27,)), dma((27,))],
        compiler_params=pltpu.CompilerParams(collective_id=1, has_side_effects=True),
        name="ghosts",
    )(payload)
    moved, leaving, centre = pl.pallas_call(
        second_kernel,
        out_shape=(
            shape((3, SEG), F32),
            shape((27, 3, 8, TILE), F32),
            shape((3, 16, 2 * TILE), F32),
        ),
        in_specs=smem(4) + vmem(8),
        out_specs=tuple(vmem(3)),
        scratch_shapes=near_scratch
        + [
            pltpu.VMEM((8, SEG), F32),
            pltpu.VMEM((768, 256), F32),
            pltpu.SMEM((PAIRS,), jnp.int32),
        ],
        compiler_params=pltpu.CompilerParams(vmem_limit_bytes=32 << 20),
        name="second",
    )(
        pair_count,
        pair_target,
        pair_source,
        pair_group,
        source,
        own,
        ghosts,
        table,
        cell,
        offset,
        force,
        node_dest,
    )
    nodes = pl.pallas_call(
        functools.partial(nodes_kernel, sizes),
        out_shape=shape((3, SEG), F32),
        in_specs=vmem(2),
        out_specs=vmem(1)[0],
        scratch_shapes=[pltpu.VMEM((27, 3, 8, TILE), F32), dma((27,)), dma((27,))],
        compiler_params=pltpu.CompilerParams(collective_id=2, has_side_effects=True),
        name="nodes",
    )(leaving, centre)
    return moved, nodes


def solution(mesh):
    sizes = tuple(mesh.shape[name] for name in ("gx", "gy", "gz"))
    whole = ("gx", "gy", "gz")
    return jax.shard_map(
        functools.partial(on_device, sizes),
        mesh=mesh,
        in_specs=(P(None, whole),) * 3 + (P(whole),) * 7 + (P(None, whole),),
        out_specs=(P(None, whole), P(None, whole)),
        check_vma=False,
    )
```

time: 819 us -> 105 us (0.13); the launches traced: 805 us -> 105 us
  other arithmetic: 320 us -> 0 us
  waiting for transfers between devices: 193 us -> 0 us
  local copies, waits for them, and re-layouts: 174 us -> 10.2 us
  Pallas kernels: 0 us -> 92.2 us
  starting transfers between devices: 82.8 us -> 0 us
  between operations: 16.8 us -> 2.1 us
  matrix products: 14.5 us -> 0 us
    scatter-add x4 -> x0, other arithmetic: 194 us -> none  [the longest x2 103 us: on_device(): jax.ops.segment_sum(values, leaving_ids, 27 * boundary + 1)[:27 * boundary]]
    psum x1 -> x0, waiting for transfers between devices: 186 us -> none  [on_device(): grid = lax.psum(grid, ('gx', 'gy', 'gz'))]
    pallas_call x0 -> x5, Pallas kernels: none -> 92.2 us  [the longest x1 35.2 us: on_device(): pl.pallas_call(functools.partial(expand_kernel, sizes), out_shape=(shape(...]
    ppermute x24 -> x0, starting transfers between devices: 82.8 us -> none  [the longest x12 50.2 us: extended(): lax.ppermute(tail, axis, [(i, (i + 1) % count) for i in range(ends)])]
    reduce_sum x58 -> x0, other arithmetic: 76.3 us -> none  [the longest x14 26.9 us: pair_force(): return jnp.sum(weight[None] * separation, axis=-1)]
    unnamed x131 -> x35, local copies, waits for them, and re-layouts: 61.2 us -> 10.2 us
    gather x30 -> x0, local copies, waits for them, and re-layouts: 38.9 us -> none  [the longest x28 37.7 us: advance(): contrib = pair_force(buffer[:, target_block], buffer[:, source_block])]
    slice x136 -> x0, local copies, waits for them, and re-layouts: 35.9 us -> none  [the longest x2 20.1 us: on_device(): jax.ops.segment_sum(values, leaving_ids, 27 * boundary + 1)[:27 * boundary]]
  transfers between devices with their start and end apart: 25 -> 0, of which waited for: 5 -> 0; matrix products, arithmetic and copies ran while one was open for 57% -> 0% of each run, Pallas kernels for 0% -> 0%
where the time goes in v1:
time: 105 us
  Pallas kernels  92.2 us (88%)
  local copies, waits for them, and re-layouts  10.2 us (10%)
  between operations  2.1 us (2%)
    pallas_call x1, Pallas kernels, on_device(): pl.pallas_call(functools.partial(expand_kernel, sizes), out_shape=(shape(...  35.2 us
    pallas_call x1, Pallas kernels, on_device(): pl.pallas_call(functools.partial(ghosts_kernel, sizes), out_shape=shape((...  19.4 us
    pallas_call x1, Pallas kernels, on_device(): pl.pallas_call(functools.partial(nodes_kernel, sizes), out_shape=shape((3...  17.7 us
    pallas_call x1, Pallas kernels, on_device(): pl.pallas_call(second_kernel, out_shape=(shape((3, SEG), F32), shape((27,...  13.5 us
    unnamed x35, local copies, waits for them, and re-layouts  10.2 us
    pallas_call x1, Pallas kernels, on_device(): pl.pallas_call(first_kernel, out_shape=(own_shape, own_shape, own_shape,...  6.43 us

profile of v1, /device:TPU:35, one launch (start us, length us, event | category | flops | bytes accessed | tf_op | source)
XLA Modules:
  0.0 104.6 jit_solution(4898173513757931980)
XLA Ops:
  0.6 0.0 copy-start.16
  0.6 0.0 copy-start.14
  0.7 0.0 copy-start.12
  2.0 0.0 copy-start.2
  2.0 0.8 copy-done.2
  2.8 0.0 copy-start.3
  2.8 0.7 copy-done.3
  3.5 0.8 copy-done.5
  4.4 0.8 copy-done.6
  5.2 0.7 copy-done.10
  5.9 35.2 %expand.1 = (f32[31,9,8,128]{3,2,1,0:T(8,128)S(1)}, f32[4,3,8,128]{3,2,1,0:T(8,128)S(1)}, f32[256,128]{1,0:T(8,128)S(1)}) custom-call(f32[3,4096]{1,0:T(4,128)S(1)} %copy-done.2, f32[3,4096]{1,0:T(4,128)S(1)} %copy-done.5, f32[3,4096]{1,0:T(4,128)S(1)} %copy-done.6, s32[32,128]{1,0:T(8,128)S(1)} %bitcast.1, s32[8]{0:T(128)S(1)} %copy-done.10, ...), custom_call_target="tpu_custom_call" | custom-call | tf_op jit(solution)/shard_map/expand/pallas_call | solution.py:691
  41.1 0.0 copy-start.11
  41.1 0.6 copy-done.11
  41.7 0.7 copy-done.13
  42.4 0.7 copy-done.15
  43.0 6.4 %first.1 = (f32[4,3,8,128]{3,2,1,0:T(8,128)S(1)}, f32[4,3,8,128]{3,2,1,0:T(8,128)S(1)}, f32[4,3,8,128]{3,2,1,0:T(8,128)S(1)}, f32[3,8,128]{2,1,0:T(8,128)S(1)}) custom-call(s32[1]{0:T(128)S(6)} %copy.15.count_ref, s32[128]{0:T(128)S(1)} %copy-done.11, s32[128]{0:T(128)S(1)} %copy-done.13, s32[128]{0:T(128)S(1)} %copy-done.15, s32[8]{0:T(128)S(1)} %copy-done.10, ...), custom_call_target="tpu_custom_call" | custom-call | tf_op jit(solution)/shard_map/first/pallas_call | solution.py:727
  49.5 0.0 copy-start.9
  49.5 0.6 copy-done.9
  50.1 19.4 %ghosts.1.ghosts_ref = f32[27,3,8,128]{3,2,1,0:T(8,128)} custom-call(f32[3,8,128]{2,1,0:T(8,128)} %copy-done.9), custom_call_target="tpu_custom_call" | custom-call | tf_op jit(solution)/shard_map/ghosts/pallas_call | solution.py:747
  69.5 0.0 copy-done.16
  69.5 0.0 copy-done.14
  69.5 0.0 copy-done.12
  69.5 0.0 copy-done.4
  69.6 0.0 copy-done.8
  69.6 0.0 copy-start
  69.6 1.0 copy-done
  70.5 13.5 %second.1 = (f32[3,4096]{1,0:T(4,128)}, f32[27,3,8,128]{3,2,1,0:T(8,128)S(1)}, f32[3,16,256]{2,1,0:T(8,128)S(1)}) custom-call(s32[1]{0:T(128)S(6)} %copy.15.count_ref, s32[128]{0:T(128)S(1)} %copy-done.12, s32[128]{0:T(128)S(1)} %copy-done.14, s32[128]{0:T(128)S(1)} %copy-done.16, f32[31,9,8,128]{3,2,1,0:T(8,128)S(1)} %get-tuple-element.12.source_ref, ...), custom_call_target="tpu_custom_call" | custom-call | tf_op jit(solution)/shard_map/second/pallas_call | solution.py:756
  84.0 0.0 copy-start.1
  84.0 0.7 copy-done.1
  84.8 0.6 copy-done.7
  85.4 17.7 %nodes.1 = f32[3,4096]{1,0:T(4,128)} custom-call(f32[27,3,8,128]{3,2,1,0:T(8,128)} %copy-done.1, f32[3,16,256]{2,1,0:T(8,128)} %copy-done.7), custom_call_target="tpu_custom_call" | custom-call | tf_op jit(solution)/shard_map/nodes/pallas_call | solution.py:787
  103.1 1.5 %copy.16 = f32[3,4096]{1,0:T(4,128)} copy(f32[3,4096]{1,0:T(4,128)} %nodes.1) | data formatting | bytes 98304
  (8 shorter events, 0.0 us)
Async XLA Ops:
  0.6 68.9 %copy-start.16 = (s32[128]{0:T(128)S(1)}, s32[128]{0:T(128)}, u32[]{:S(2)}) copy-start(s32[128]{0:T(128)} %group_ref.3) | copy-start | bytes 1540
  0.6 68.9 %copy-start.14 = (s32[128]{0:T(128)S(1)}, s32[128]{0:T(128)}, u32[]{:S(2)}) copy-start(s32[128]{0:T(128)} %from_ref.3) | copy-start | bytes 1540
  0.7 68.9 %copy-start.12 = (s32[128]{0:T(128)S(1)}, s32[128]{0:T(128)}, u32[]{:S(2)}) copy-start(s32[128]{0:T(128)} %target_ref.3) | copy-start | bytes 1540
  2.0 0.8 copy-start.2
  2.8 0.7 copy-start.3
  3.5 0.8 copy-start.5
  4.4 0.8 copy-start.6
  5.2 0.7 copy-start.10
  5.9 63.7 %copy-start.4 = (s32[4096]{0:T(1024)S(1)}, s32[4096]{0:T(1024)}, u32[]{:S(2)}) copy-start(s32[4096]{0:T(1024)} %param.14) | copy-start | bytes 49156
  5.9 63.7 %copy-start.8 = (s32[2,4096]{1,0:T(2,128)S(1)}, s32[2,4096]{1,0:T(2,128)}, u32[]{:S(2)}) copy-start(s32[2,4096]{1,0:T(2,128)} %dest_ref.1) | copy-start | bytes 98308
  41.1 0.7 copy-start.11
  41.7 0.7 copy-start.13
  42.4 0.7 copy-start.15
  49.5 0.6 copy-start.9
  69.6 1.0 copy-start
  84.0 0.7 copy-start.1
  84.8 0.6 copy-start.7

commit v2 on v1

v2 whole, which is shorter than its diff:
```python
import functools

import jax
import jax.numpy as jnp
from jax import lax
from jax.experimental import pallas as pl
from jax.experimental.pallas import tpu as pltpu
from jax.sharding import PartitionSpec as P

TILE = 128
SEG = 4096
GROUPS = 4
GHOST_DEV = 8
CELL_DEV = 16
COMP = 6
TERMS = 35
LANE_STEP = 42
PAIRS = 128
CORE2 = 0.25
NEAR_SCALE = 0.05
FAR_SCALE = 0.002
STEP_SIZE = 0.1
MESH = pl.DeviceIdType.MESH
F32 = jnp.float32
BF16 = jnp.bfloat16
EXPONENTS = [
    (a, b, degree - a - b)
    for degree in range(5)
    for a in range(degree, -1, -1)
    for b in range(degree - a, -1, -1)
]
NT = (((1,), (1,)), ((), ()))
TN = (((0,), (0,)), ((), ()))


def vmem(count):
    return [pl.BlockSpec(memory_space=pltpu.VMEM)] * count


def smem(count):
    return [pl.BlockSpec(memory_space=pltpu.SMEM)] * count


def halves_of(value):
    high = value.astype(BF16).astype(F32)
    return high, value - high


def powers(unit):
    square = unit * unit
    return [None, unit, square, square * unit, square * square]


def monomial(u, v, w, exps):
    result = None
    for table, power in zip((u, v, w), exps):
        if power:
            result = table[power] if result is None else result * table[power]
    return result


def symmetric(b, t):
    return [
        b[0] * t[0],
        b[1] * t[1],
        b[2] * t[2],
        0.5 * (b[0] * t[1] + b[1] * t[0]),
        0.5 * (b[1] * t[2] + b[2] * t[1]),
        0.5 * (b[0] * t[2] + b[2] * t[0]),
    ]


class Place:
    def __init__(self, sizes):
        self.sizes = sizes
        self.at = tuple(lax.axis_index(name) for name in ("gx", "gy", "gz"))

    def beside(self, slot, sign=1):
        steps = (slot // 9 - 1, slot // 3 % 3 - 1, slot % 3 - 1)
        where = tuple(a + sign * s for a, s in zip(self.at, steps))
        inside = slot != 13
        for at, size in zip(where, self.sizes):
            inside = jnp.logical_and(inside, jnp.logical_and(at >= 0, at < size))
        return where, inside

    def count_beside(self):
        total = 1
        for at, size in zip(self.at, self.sizes):
            total = total * (3 - (at == 0).astype(jnp.int32) - (at == size - 1).astype(jnp.int32))
        return total - 1


def each_slot(body):
    def step(slot, carry):
        body(slot)
        return carry

    lax.fori_loop(0, 27, step, 0)


def greet_neighbours(place, barrier):
    def greet(slot):
        where, inside = place.beside(slot)

        @pl.when(inside)
        def _():
            pl.semaphore_signal(barrier, inc=1, device_id=where, device_id_type=MESH)

    each_slot(greet)


def far_force(offset, burg, line, cell, table_ref):
    u, v, w = (powers(2.0 * value) for value in offset)
    stress = [None] * COMP
    for at, exps in enumerate(EXPONENTS):
        value = monomial(u, v, w, exps)
        for comp in range(COMP):
            row = comp // 3 * TILE + comp % 3 * LANE_STEP + at
            entry = jnp.broadcast_to(table_ref[pl.ds(row, 1), :], (8, TILE))
            term = jnp.take_along_axis(entry, cell, axis=1, mode="promise_in_bounds")
            if value is not None:
                term = term * value
            stress[comp] = term if stress[comp] is None else stress[comp] + term
    push_x = stress[0] * burg[0] + stress[3] * burg[1] + stress[5] * burg[2]
    push_y = stress[3] * burg[0] + stress[1] * burg[1] + stress[4] * burg[2]
    push_z = stress[5] * burg[0] + stress[4] * burg[1] + stress[2] * burg[2]
    return [
        push_y * line[2] - push_z * line[1],
        push_z * line[0] - push_x * line[2],
        push_x * line[1] - push_y * line[0],
    ]


def exchange(place, send_of, receive_at, send_sem, recv_sem):
    def copy_of(slot):
        where, inside = place.beside(slot)
        copy = pltpu.make_async_remote_copy(
            src_ref=send_of(slot),
            dst_ref=receive_at(26 - slot),
            send_sem=send_sem.at[slot],
            recv_sem=recv_sem.at[26 - slot],
            device_id=where,
            device_id_type=MESH,
        )
        return copy, inside

    def start(slot):
        copy, inside = copy_of(slot)

        @pl.when(inside)
        def _():
            copy.start()

    def wait(slot):
        copy, inside = copy_of(slot)

        @pl.when(inside)
        def _():
            copy.wait_send()

        arriving, _ = copy_of(26 - slot)

        @pl.when(inside)
        def _():
            arriving.wait_recv()

    return start, wait


SIDE = 48 * 8
ACROSS = 80 * 8
UNROLL = 8
WIDTH = 512


def pieces_of(value):
    high = value.astype(BF16).astype(F32)
    rest = value - high
    middle = rest.astype(BF16).astype(F32)
    return [high, middle, rest - middle]


def product_halves(burg, line):
    highs, lows = [], []
    for b in burg:
        for t in line:
            high, low = halves_of(b * t)
            highs.append(high)
            lows.append(low)
    return highs, lows


def store_rows(ref, at, rows):
    for row, value in enumerate(rows):
        ref[pl.ds(at + 8 * row, 8), :] = value


def fill_strengths(sides, group, burg, line):
    highs, lows = product_halves(burg, line)
    zero, one = jnp.zeros((8, TILE), F32), jnp.ones((8, TILE), F32)
    at = pl.multiple_of(group * SIDE, SIDE)
    store_rows(sides, at, highs + highs + lows + [zero] * 5)
    store_rows(sides, at + 41 * 8, [one] * 3 + [zero] * 4)


def fill_places(sides, group, places):
    at = pl.multiple_of(group * SIDE, SIDE)
    store_rows(sides, at + 32 * 8, [piece for place in places for piece in pieces_of(place)])


def fill_across_strengths(across, group, burg, line):
    highs, lows = product_halves(burg, line)
    zero = jnp.zeros((8, TILE), F32)
    store_rows(across, group * ACROSS, highs + lows + highs + [zero] * 5)


def fill_across_places(across, group, places):
    zero, one = jnp.zeros((8, TILE), F32), jnp.ones((8, TILE), F32)
    for row in range(3):
        signs = [-one if at // 3 == row else zero for at in range(9)]
        store_rows(
            across,
            group * ACROSS + (32 + 16 * row) * 8,
            signs + pieces_of(places[row]) + [zero] * 4,
        )


def fill_targets(across, targets, strengths):
    def fill(tile, carry):
        at = tile // 8 * ACROSS + tile % 8
        if strengths:
            top = across[pl.ds(at, 32, stride=8), :]
            zero = jnp.zeros((32, 3 * TILE), F32)
            targets[tile, pl.ds(0, 32), :] = jnp.concatenate([top, zero], axis=1).astype(BF16)
        low = [across[pl.ds(at + (32 + 16 * row) * 8, 16, stride=8), :] for row in range(3)]
        low = jnp.concatenate([jnp.zeros((16, TILE), F32)] + low, axis=1)
        targets[tile, pl.ds(32, 16), :] = low.astype(BF16)
        return carry

    lax.fori_loop(0, SEG // TILE, fill, 0)


def near_pass(sweep, live, target_ref, from_ref, target_row, group_row, sides, targets, pairs, near):
    def forces_of_pair(pair):
        source = from_ref[pair]
        left = sides[pl.ds((source >> 3) * SIDE + (source & 7), 48, stride=8), :]
        both = lax.dot_general(
            left.astype(BF16), targets[target_ref[pair]], TN, preferred_element_type=F32
        )
        totals = [jnp.zeros((8, TILE), F32)] * 3
        for chunk in range(16):
            span = both[8 * chunk : 8 * chunk + 8]
            gaps = [span[:, TILE * (row + 1) : TILE * (row + 2)] for row in range(3)]
            radius2 = gaps[0] * gaps[0] + gaps[1] * gaps[1] + gaps[2] * gaps[2] + CORE2
            inverse = lax.rsqrt(radius2)
            weight = span[:, :TILE] * (inverse * inverse * inverse)
            totals = [total + weight * gap for total, gap in zip(totals, gaps)]
        return totals

    def step(block, carry):
        results = [forces_of_pair(block * UNROLL + at) for at in range(UNROLL)]
        for row in range(3):
            rows = [jnp.sum(totals[row], axis=0, keepdims=True) for totals in results]
            at = pl.multiple_of(row * PAIRS + block * UNROLL, UNROLL)
            pairs[pl.ds(at, UNROLL), :] = jnp.concatenate(rows, axis=0)
        return carry

    lax.fori_loop(0, PAIRS // UNROLL, step, 0)
    tile_ids = lax.broadcasted_iota(jnp.int32, (SEG // TILE, PAIRS), 0)
    pair_ids = lax.broadcasted_iota(jnp.int32, (SEG // TILE, PAIRS), 1)
    wanted = (tile_ids == target_row) & (group_row == sweep) & (pair_ids < live)
    select = jnp.where(wanted, 1.0, 0.0).astype(BF16)
    for row in range(3):
        total = None
        for piece in pieces_of(pairs[pl.ds(row * PAIRS, PAIRS), :]):
            part = jnp.dot(select, piece.astype(BF16), preferred_element_type=F32)
            total = part if total is None else total + part
        near[pl.ds(32 * row, 32), :] = total


def step_kernel(
    sizes,
    ghost_ref,
    live_ref,
    count_ref,
    target_ref,
    from_ref,
    rel_hbm,
    burg_hbm,
    line_hbm,
    cell_hbm,
    dest_hbm,
    target_hbm,
    group_hbm,
    moved_ref,
    nodes_ref,
    rel_ref,
    burg_ref,
    line_ref,
    cell_ref,
    dest_ref,
    target_row,
    group_row,
    own,
    base,
    offset,
    force,
    far,
    payload,
    landing,
    payload_next,
    landing_next,
    mono,
    symm,
    gathered,
    contrib,
    arrived,
    table_ref,
    sides,
    across,
    targets,
    pairs,
    near,
    values,
    lowers,
    centre,
    sums,
    leaving,
    landed,
    load_sem,
    ghost_send,
    ghost_recv,
    next_send,
    next_recv,
    node_send,
    node_recv,
    plane_send,
    plane_recv,
    line_send,
    line_recv,
):
    loads = [
        pltpu.make_async_copy(source, target, load_sem.at[at])
        for at, (source, target) in enumerate(
            [
                (rel_hbm, rel_ref),
                (burg_hbm, burg_ref),
                (line_hbm, line_ref),
                (cell_hbm, cell_ref),
                (dest_hbm, dest_ref),
                (target_hbm, target_row),
                (group_hbm, group_row),
            ]
        )
    ]
    for load in loads:
        load.start()
    nx, ny, nz = sizes
    plane = ny * nz
    place = Place(sizes)
    gx, gy, gz = place.at
    here = gy * nz + gz

    def plane_peer(step):
        peer = lax.rem(here + step, plane)
        return (gx, peer // nz, lax.rem(peer, nz))

    def line_peer(step):
        return (lax.rem(gx + step, nx), gy, gz)

    barrier = pltpu.get_barrier_semaphore()
    greet_neighbours(place, barrier)

    def greet_plane(step, carry):
        pl.semaphore_signal(barrier, inc=1, device_id=plane_peer(step), device_id_type=MESH)
        return carry

    def greet_line(step, carry):
        pl.semaphore_signal(barrier, inc=1, device_id=line_peer(step), device_id_type=MESH)
        return carry

    lax.fori_loop(1, plane, greet_plane, 0)
    lax.fori_loop(1, nx, greet_line, 0)

    for load in loads:
        load.wait()
    for tile in range(SEG // TILE):
        lanes = pl.ds(tile * TILE, TILE)
        for row in range(3):
            own[tile // 8, row, pl.ds(tile % 8, 1), :] = rel_ref[pl.ds(row, 1), lanes]
            own[tile // 8, 3 + row, pl.ds(tile % 8, 1), :] = burg_ref[pl.ds(row, 1), lanes]
            own[tile // 8, 6 + row, pl.ds(tile % 8, 1), :] = line_ref[pl.ds(row, 1), lanes]
    for group in range(GROUPS):
        rows = slice(8 * group, 8 * group + 8)
        cell = cell_ref[rows, :]
        rel = [own[group, row] for row in range(3)]
        burg = [own[group, 3 + row] for row in range(3)]
        line = [own[group, 6 + row] for row in range(3)]
        corner = (
            jnp.full((8, TILE), gx, jnp.int32),
            gy * 4 + (cell >> 2),
            gz * 4 + (cell & 3),
        )
        for row in range(3):
            corner_row = corner[row].astype(F32) + 0.5
            base[group, row] = corner_row
            offset[group, row] = rel[row]
            own[group, row] = corner_row + rel[row]
        for at, value in enumerate(symmetric(burg, line)):
            symm[pl.ds(at * 32 + 8 * group, 8), :] = value
        u, v, w = (powers(2.0 * value) for value in rel)
        for at, exps in enumerate(EXPONENTS):
            value = monomial(u, v, w, exps)
            mono[pl.ds(at * 32 + 8 * group, 8), :] = (
                jnp.ones((8, TILE), F32) if value is None else value
            )
    for at in range(TERMS, 40):
        mono[pl.ds(at * 32, 32), :] = jnp.zeros((32, TILE), F32)
    for ghost in range(GHOST_DEV):
        tile = ghost_ref[ghost]
        live = jnp.where(ghost < live_ref[0], 1.0, 0.0)
        for row in range(9):
            value = own[tile // 8, row, pl.ds(lax.rem(tile, 8), 1), :]
            payload[row, pl.ds(ghost, 1), :] = value * live

    cells = lax.broadcasted_iota(jnp.int32, (CELL_DEV, TILE), 0)
    moments = jnp.zeros((COMP * CELL_DEV, 40), F32)
    for block in range(4):
        lefts, rights = [], []
        for tile in range(8 * block, 8 * block + 8):
            chosen = cells == cell_ref[pl.ds(tile, 1), :]
            left = jnp.concatenate(
                [
                    jnp.where(chosen, symm[pl.ds(at * 32 + tile, 1), :], 0.0)
                    for at in range(COMP)
                ],
                axis=0,
            )
            right = mono[pl.ds(tile, 40, stride=32), :]
            left_high, left_low = halves_of(left)
            right_high, right_low = halves_of(right)
            lefts += [left_high, left_high, left_low]
            rights += [right_high, right_low, right_high]
        moments = moments + lax.dot_general(
            jnp.concatenate(lefts, axis=1).astype(BF16),
            jnp.concatenate(rights, axis=1).astype(BF16),
            NT,
            preferred_element_type=F32,
        )
    wide = jnp.concatenate([moments, jnp.zeros((COMP * CELL_DEV, TILE - 40), F32)], axis=1)
    mine = pl.ds(pl.multiple_of(here * CELL_DEV, CELL_DEV), CELL_DEV)
    for half in range(2):
        total = jnp.zeros((CELL_DEV, TILE), F32)
        for third in range(3):
            at = (3 * half + third) * CELL_DEV
            part = wide[at : at + CELL_DEV]
            total = total + (pltpu.roll(part, third * LANE_STEP, 1) if third else part)
        gathered[mine, pl.ds(half * TILE, TILE)] = total

    pl.semaphore_wait(barrier, place.count_beside() + plane - 1 + nx - 1)

    def plane_copy(step):
        return pltpu.make_async_remote_copy(
            src_ref=gathered.at[mine],
            dst_ref=gathered.at[mine],
            send_sem=plane_send.at[step],
            recv_sem=plane_recv.at[step],
            device_id=plane_peer(step),
            device_id_type=MESH,
        )

    def ghost_copy(slot):
        where, inside = place.beside(slot)
        copy = pltpu.make_async_remote_copy(
            src_ref=payload,
            dst_ref=landing.at[26 - slot],
            send_sem=ghost_send.at[slot],
            recv_sem=ghost_recv.at[26 - slot],
            device_id=where,
            device_id_type=MESH,
        )
        return copy, inside

    def start_plane(step, carry):
        plane_copy(step).start()
        return carry

    lax.fori_loop(1, plane, start_plane, 0)

    def start_ghost(slot):
        copy, inside = ghost_copy(slot)

        @pl.when(inside)
        def _():
            copy.start()

    each_slot(start_ghost)

    def clear(slot):
        _, inside = place.beside(slot)

        @pl.when(jnp.logical_not(inside))
        def _():
            landed[slot] = jnp.zeros((3, 8, TILE), F32)

    each_slot(clear)

    for group in range(GROUPS):
        places = [own[group, row] for row in range(3)]
        burg = [own[group, 3 + row] for row in range(3)]
        line = [own[group, 6 + row] for row in range(3)]
        fill_strengths(sides, group, burg, line)
        fill_places(sides, group, places)
        fill_across_strengths(across, group, burg, line)
        fill_across_places(across, group, places)
    fill_targets(across, targets, True)
    rows, columns = nx * CELL_DEV, plane * CELL_DEV
    row = lax.broadcasted_iota(jnp.int32, (rows, columns), 0)
    column = lax.broadcasted_iota(jnp.int32, (rows, columns), 1)
    peer = column >> 4
    step_x = (row >> 4) - gx
    step_y = gy * 4 + ((row >> 2) & 3) - (peer // nz * 4 + ((column >> 2) & 3))
    step_z = gz * 4 + (row & 3) - (peer % nz * 4 + (column & 3))
    distance2 = (step_x * step_x + step_y * step_y + step_z * step_z).astype(F32)
    weight = jnp.where(distance2 > 3.5, 1.0 / jnp.sqrt(jnp.maximum(distance2, 1.0)), 0.0)

    def wait_plane(step, carry):
        plane_copy(step).wait()
        return carry

    lax.fori_loop(1, plane, wait_plane, 0)
    contrib[...] = jnp.dot(
        weight, gathered[...], precision=lax.Precision.HIGHEST, preferred_element_type=F32
    )

    def line_copy(step):
        there = lax.rem(gx + step, nx)
        return pltpu.make_async_remote_copy(
            src_ref=contrib.at[pl.ds(pl.multiple_of(there * CELL_DEV, CELL_DEV), CELL_DEV)],
            dst_ref=arrived.at[step],
            send_sem=line_send.at[step],
            recv_sem=line_recv.at[step],
            device_id=line_peer(step),
            device_id_type=MESH,
        )

    def start_line(step, carry):
        line_copy(step).start()
        return carry

    lax.fori_loop(1, nx, start_line, 0)
    def take_ghosts(slot):
        copy, _ = ghost_copy(26 - slot)
        _, inside = place.beside(slot)

        @pl.when(inside)
        def _():
            copy.wait_recv()
            block = [landing[slot, row] for row in range(9)]
            fill_strengths(sides, GROUPS + slot, block[3:6], block[6:9])
            fill_places(sides, GROUPS + slot, block[0:3])

        @pl.when(jnp.logical_not(inside))
        def _():
            nothing = [jnp.zeros((8, TILE), F32)] * 3
            fill_strengths(sides, GROUPS + slot, nothing, nothing)
            fill_places(sides, GROUPS + slot, nothing)

    each_slot(take_ghosts)
    live = count_ref[0]
    near_pass(
        0, live, target_ref, from_ref, target_row[...], group_row[...], sides, targets, pairs, near
    )
    total = contrib[pl.ds(pl.multiple_of(gx * CELL_DEV, CELL_DEV), CELL_DEV), :]

    def wait_line(step, carry):
        line_copy(step).wait()
        return carry

    lax.fori_loop(1, nx, wait_line, 0)
    for step in range(1, nx):
        total = total + arrived[step]
    full = jnp.concatenate([total, jnp.zeros((TILE - CELL_DEV, 2 * TILE), F32)], axis=0)
    table_ref[pl.ds(0, TILE), :] = full[:, :TILE].T
    table_ref[pl.ds(TILE, TILE), :] = full[:, TILE:].T
    def far_pass(group):
        return far_force(
            [offset[group, row] for row in range(3)],
            [own[group, 3 + row] for row in range(3)],
            [own[group, 6 + row] for row in range(3)],
            cell_ref[pl.ds(8 * group, 8), :],
            table_ref,
        )

    for group in range(GROUPS):
        coupling = far_pass(group)
        for row in range(3):
            total = FAR_SCALE * coupling[row] + NEAR_SCALE * near[pl.ds(32 * row + 8 * group, 8), :]
            moved = offset[group, row] + STEP_SIZE * total
            force[group, row] = total
            offset[group, row] = moved
            own[group, row] = base[group, row] + moved
    for ghost in range(GHOST_DEV):
        tile = ghost_ref[ghost]
        for row in range(3):
            payload_next[row, pl.ds(ghost, 1), :] = own[tile // 8, row, pl.ds(lax.rem(tile, 8), 1), :]
    start_next, wait_next = exchange(
        place, lambda slot: payload_next, lambda slot: landing_next.at[slot], next_send, next_recv
    )
    each_slot(start_next)

    for group in range(GROUPS):
        coupling = far_pass(group)
        for row in range(3):
            far[group, row] = coupling[row]
        places = [own[group, row] for row in range(3)]
        fill_places(sides, group, places)
        fill_across_places(across, group, places)
    fill_targets(across, targets, False)
    low_ids = lax.broadcasted_iota(jnp.int32, (256, WIDTH), 0)

    def fill_lowers(block, carry):
        lanes = pl.ds(pl.multiple_of(block * WIDTH, WIDTH), WIDTH)
        for end in range(2):
            lower = dest_ref[pl.ds(end, 1), lanes] & 255
            lowers[block, end] = jnp.where(low_ids == lower, 1.0, 0.0).astype(BF16)
        return carry

    lax.fori_loop(0, SEG // WIDTH, fill_lowers, 0)

    def take_next(slot):
        wait_next(slot)
        _, inside = place.beside(slot)

        @pl.when(inside)
        def _():
            fill_places(sides, GROUPS + slot, [landing_next[slot, row] for row in range(3)])

    each_slot(take_next)
    near_pass(
        1, live, target_ref, from_ref, target_row[...], group_row[...], sides, targets, pairs, near
    )
    for group in range(GROUPS):
        for row in range(3):
            total = FAR_SCALE * far[group, row] + NEAR_SCALE * near[pl.ds(32 * row + 8 * group, 8), :]
            moved = offset[group, row] + STEP_SIZE * total
            half = 0.5 * (force[group, row] + total)
            for tile in range(8):
                lanes = pl.ds((8 * group + tile) * TILE, TILE)
                moved_ref[pl.ds(row, 1), lanes] = moved[tile : tile + 1]
                values[pl.ds(row, 1), lanes] = half[tile : tile + 1]

    def scatter(first, count, totals):
        totals[...] = jnp.zeros(totals.shape, F32)
        high_ids = lax.broadcasted_iota(jnp.int32, (count, WIDTH), 0) + first

        def add(block, carry):
            lanes = pl.ds(pl.multiple_of(block * WIDTH, WIDTH), WIDTH)
            parts = [halves_of(values[pl.ds(row, 1), lanes]) for row in range(3)]
            for end in range(2):
                dest = dest_ref[pl.ds(end, 1), lanes]
                slot = dest >> 12
                upper = jnp.where(slot == 13, 0, 16 + 4 * slot) + ((dest & (SEG - 1)) >> 8)
                chosen = high_ids == upper
                left = jnp.concatenate(
                    [
                        jnp.where(chosen, parts[row][piece], 0.0).astype(BF16)
                        for row in range(3)
                        for piece in range(2)
                    ],
                    axis=0,
                )
                totals[...] += lax.dot_general(
                    left, lowers[block, end], NT, preferred_element_type=F32
                )
            return carry

        lax.fori_loop(0, SEG // WIDTH, add, 0)

    scatter(16, 112, sums)
    for row in range(3):
        for slot in range(27):
            at = 224 * row + 4 * slot
            both = sums[pl.ds(at, 4), :] + sums[pl.ds(at + 112, 4), :]
            leaving[slot, row, pl.ds(0, 4), :] = both[:, :TILE]
            leaving[slot, row, pl.ds(4, 4), :] = both[:, TILE:]
    start_node, wait_node = exchange(
        place, lambda slot: leaving.at[slot], lambda slot: landed.at[slot], node_send, node_recv
    )
    each_slot(start_node)
    scatter(0, 16, centre)
    middle = [
        centre[pl.ds(32 * row, 16), :] + centre[pl.ds(32 * row + 16, 16), :] for row in range(3)
    ]
    for row in range(3):
        for part in range(4, 16):
            nodes_ref[pl.ds(row, 1), pl.ds(256 * part, 256)] = middle[row][part : part + 1]
    each_slot(wait_node)
    for row in range(3):
        total = landed[0, row]
        for slot in range(1, 27):
            total = total + landed[slot, row]
        for part in range(4):
            for half in range(2):
                lanes = slice(TILE * half, TILE * half + TILE)
                nodes_ref[pl.ds(row, 1), pl.ds(256 * part + TILE * half, TILE)] = (
                    middle[row][part : part + 1, lanes]
                    + total[4 * half + part : 4 * half + part + 1]
                )

    def wait_ghost_send(slot):
        copy, inside = ghost_copy(slot)

        @pl.when(inside)
        def _():
            copy.wait_send()

    each_slot(wait_ghost_send)


def on_device(
    sizes,
    seg_rel,
    burgers,
    line_vec,
    seg_cell,
    ghost_tiles,
    ghost_count,
    pair_target,
    pair_source,
    pair_group,
    pair_count,
    node_dest,
):
    nx, ny, nz = sizes
    plane = ny * nz
    cell = seg_cell.reshape(SEG // TILE, TILE)
    shape = jax.ShapeDtypeStruct
    dma = pltpu.SemaphoreType.DMA
    block = (GROUPS, 3, 8, TILE)
    buffers = [
        (3, SEG),
        (3, SEG),
        (3, SEG),
        (SEG // TILE, TILE, jnp.int32),
        (2, SEG, jnp.int32),
        (1, PAIRS, jnp.int32),
        (1, PAIRS, jnp.int32),
        (GROUPS, 9, 8, TILE),
        block,
        block,
        block,
        block,
        (9, GHOST_DEV, TILE),
        (27, 9, GHOST_DEV, TILE),
        (3, GHOST_DEV, TILE),
        (27, 3, GHOST_DEV, TILE),
        (40 * 32, TILE),
        (COMP * 32, TILE),
        (plane * CELL_DEV, 2 * TILE),
        (nx * CELL_DEV, 2 * TILE),
        (nx, CELL_DEV, 2 * TILE),
        (2 * TILE, TILE),
        ((GROUPS + 27) * SIDE, TILE),
        (GROUPS * ACROSS, TILE),
        (SEG // TILE, 48, 4 * TILE, BF16),
        (3 * PAIRS, TILE),
        (3 * SEG // TILE, TILE),
        (8, SEG),
        (SEG // WIDTH, 2, 256, WIDTH, BF16),
        (96, 256),
        (672, 256),
        (27, 3, 8, TILE),
        (27, 3, 8, TILE),
    ]
    scratch = []
    for sides in buffers:
        kind = F32
        if not isinstance(sides[-1], int):
            sides, kind = sides[:-1], sides[-1]
        scratch.append(pltpu.VMEM(sides, kind))
    return pl.pallas_call(
        functools.partial(step_kernel, sizes),
        out_shape=(shape((3, SEG), F32), shape((3, SEG), F32)),
        in_specs=smem(5) + [pl.BlockSpec(memory_space=pl.ANY)] * 7,
        out_specs=tuple(vmem(2)),
        scratch_shapes=scratch
        + [dma((7,))]
        + [dma((27,))] * 6
        + [dma((plane,))] * 2
        + [dma((nx,))] * 2,
        compiler_params=pltpu.CompilerParams(
            collective_id=0, has_side_effects=True, vmem_limit_bytes=56 << 20
        ),
        name="step",
    )(
        ghost_tiles,
        ghost_count,
        pair_count,
        pair_target,
        pair_source,
        seg_rel,
        burgers,
        line_vec,
        cell,
        node_dest,
        pair_target.reshape(1, PAIRS),
        pair_group.reshape(1, PAIRS),
    )


def solution(mesh):
    sizes = tuple(mesh.shape[name] for name in ("gx", "gy", "gz"))
    whole = ("gx", "gy", "gz")
    return jax.shard_map(
        functools.partial(on_device, sizes),
        mesh=mesh,
        in_specs=(P(None, whole),) * 3 + (P(whole),) * 7 + (P(None, whole),),
        out_specs=(P(None, whole), P(None, whole)),
        check_vma=False,
    )
```

time: 105 us -> 70.5 us (0.67)
  Pallas kernels: 92.2 us -> 66.3 us
  local copies, waits for them, and re-layouts: 10.2 us -> 2.15 us
    pallas_call x5 -> x1, Pallas kernels: 92.2 us -> 66.3 us  [on_device(): pl.pallas_call(functools.partial(step_kernel, sizes), out_shape=(shape((3...]
    unnamed x35 -> x4, local copies, waits for them, and re-layouts: 10.2 us -> 2.15 us
where the time goes in v2:
time: 70.5 us; the launch traced here: 70.3 us
  Pallas kernels  66.3 us (94%)
  local copies, waits for them, and re-layouts  2.15 us (3%)
  between operations  1.94 us (3%)
    pallas_call x1, Pallas kernels, on_device(): pl.pallas_call(functools.partial(step_kernel, sizes), out_shape=(shape((3...  66.3 us
    unnamed x4, local copies, waits for them, and re-layouts  2.15 us

profile of v2, /device:TPU:35, one launch (start us, length us, event | category | flops | bytes accessed | tf_op | source)
XLA Modules:
  0.0 70.3 jit_solution(13206110002371378826)
XLA Ops:
  1.9 66.3 %step.1 = (f32[3,4096]{1,0:T(4,128)}, f32[3,4096]{1,0:T(4,128)}) custom-call(s32[8]{0:T(128)} %ghost_ref.1, s32[1]{0:T(128)S(6)} %copy.15.live_ref, s32[1]{0:T(128)S(6)} %copy.16.count_ref, s32[128]{0:T(128)} %target_ref.1, s32[128]{0:T(128)} %from_ref.1, f32[3,4096]{1,0:T(4,128)} %rel_hbm.1, f32[3,4096]{1,0:T(4,128)} %burg_hbm.1, f32[3,4096]{1,0:T(4,128)} %line_hbm.1, ...), custom_call_target="tpu_custom_call" | custom-call | tf_op jit(solution)/shard_map/step/pallas_call | solution.py:782
  68.2 0.0 copy-start
  68.2 1.5 %copy.17 = f32[3,4096]{1,0:T(4,128)} copy(f32[3,4096]{1,0:T(4,128)} %get-tuple-element.4) | data formatting | bytes 98304
  69.7 0.0 copy-done
  69.7 0.6 copy.18
Async XLA Ops:
  68.2 1.5 %copy-start = (f32[3,4096]{1,0:T(4,128)S(1)}, f32[3,4096]{1,0:T(4,128)}, u32[]{:S(2)}) copy-start(f32[3,4096]{1,0:T(4,128)} %get-tuple-element.5) | copy-start | bytes 147460

commit v3 on v2

--- a/solution.py
+++ b/solution.py
@@ -74,13 +74,17 @@
     def __init__(self, sizes):
         self.sizes = sizes
         self.at = tuple(lax.axis_index(name) for name in ("gx", "gy", "gz"))
-
-    def beside(self, slot, sign=1):
+        self.free = [
+            {-1: at > 0, 1: at < size - 1} for at, size in zip(self.at, sizes)
+        ]
+
+    def beside(self, slot):
         steps = (slot // 9 - 1, slot // 3 % 3 - 1, slot % 3 - 1)
-        where = tuple(a + sign * s for a, s in zip(self.at, steps))
-        inside = slot != 13
-        for at, size in zip(where, self.sizes):
-            inside = jnp.logical_and(inside, jnp.logical_and(at >= 0, at < size))
+        where = tuple(at + step for at, step in zip(self.at, steps))
+        inside = None
+        for free, step in zip(self.free, steps):
+            if step:
+                inside = free[step] if inside is None else jnp.logical_and(inside, free[step])
         return where, inside
 
     def count_beside(self):
@@ -91,11 +95,9 @@
 
 
 def each_slot(body):
-    def step(slot, carry):
-        body(slot)
-        return carry
-
-    lax.fori_loop(0, 27, step, 0)
+    for slot in range(27):
+        if slot != 13:
+            body(slot)
 
 
 def greet_neighbours(place, barrier):
@@ -152,24 +154,26 @@
             copy.start()
 
     def wait(slot):
+        arriving, _ = copy_of(26 - slot)
+        _, inside = place.beside(slot)
+
+        @pl.when(inside)
+        def _():
+            arriving.wait_recv()
+
+    def wait_sent(slot):
         copy, inside = copy_of(slot)
 
         @pl.when(inside)
         def _():
             copy.wait_send()
 
-        arriving, _ = copy_of(26 - slot)
-
-        @pl.when(inside)
-        def _():
-            arriving.wait_recv()
-
-    return start, wait
+    return start, wait, wait_sent
 
 
 SIDE = 48 * 8
 ACROSS = 80 * 8
-UNROLL = 8
+UNROLL = 16
 WIDTH = 512
 
 
@@ -362,11 +366,14 @@
     here = gy * nz + gz
 
     def plane_peer(step):
-        peer = lax.rem(here + step, plane)
-        return (gx, peer // nz, lax.rem(peer, nz))
+        peer = here + step
+        peer = jnp.where(peer >= plane, peer - plane, peer)
+        row = sum((peer >= nz * at).astype(jnp.int32) for at in range(1, ny))
+        return (gx, row, peer - nz * row)
 
     def line_peer(step):
-        return (lax.rem(gx + step, nx), gy, gz)
+        there = gx + step
+        return (jnp.where(there >= nx, there - nx, there), gy, gz)
 
     barrier = pltpu.get_barrier_semaphore()
     greet_neighbours(place, barrier)
@@ -501,9 +508,13 @@
 
         @pl.when(jnp.logical_not(inside))
         def _():
+            landing[slot] = jnp.zeros((9, GHOST_DEV, TILE), F32)
+            landing_next[slot] = jnp.zeros((3, GHOST_DEV, TILE), F32)
             landed[slot] = jnp.zeros((3, 8, TILE), F32)
 
     each_slot(clear)
+    landing[13] = jnp.zeros((9, GHOST_DEV, TILE), F32)
+    landing_next[13] = jnp.zeros((3, GHOST_DEV, TILE), F32)
 
     for group in range(GROUPS):
         places = [own[group, row] for row in range(3)]
@@ -534,7 +545,7 @@
     )
 
     def line_copy(step):
-        there = lax.rem(gx + step, nx)
+        there = line_peer(step)[0]
         return pltpu.make_async_remote_copy(
             src_ref=contrib.at[pl.ds(pl.multiple_of(there * CELL_DEV, CELL_DEV), CELL_DEV)],
             dst_ref=arrived.at[step],
@@ -549,24 +560,22 @@
         return carry
 
     lax.fori_loop(1, nx, start_line, 0)
-    def take_ghosts(slot):
+    def wait_ghost(slot):
         copy, _ = ghost_copy(26 - slot)
         _, inside = place.beside(slot)
 
         @pl.when(inside)
         def _():
             copy.wait_recv()
-            block = [landing[slot, row] for row in range(9)]
-            fill_strengths(sides, GROUPS + slot, block[3:6], block[6:9])
-            fill_places(sides, GROUPS + slot, block[0:3])
-
-        @pl.when(jnp.logical_not(inside))
-        def _():
-            nothing = [jnp.zeros((8, TILE), F32)] * 3
-            fill_strengths(sides, GROUPS + slot, nothing, nothing)
-            fill_places(sides, GROUPS + slot, nothing)
-
-    each_slot(take_ghosts)
+
+    def take_ghosts(slot, carry):
+        block = [landing[slot, row] for row in range(9)]
+        fill_strengths(sides, GROUPS + slot, block[3:6], block[6:9])
+        fill_places(sides, GROUPS + slot, block[0:3])
+        return carry
+
+    each_slot(wait_ghost)
+    lax.fori_loop(0, 27, take_ghosts, 0)
     live = count_ref[0]
     near_pass(
         0, live, target_ref, from_ref, target_row[...], group_row[...], sides, targets, pairs, near
@@ -604,7 +613,7 @@
         tile = ghost_ref[ghost]
         for row in range(3):
             payload_next[row, pl.ds(ghost, 1), :] = own[tile // 8, row, pl.ds(lax.rem(tile, 8), 1), :]
-    start_next, wait_next = exchange(
+    start_next, wait_next, wait_next_sent = exchange(
         place, lambda slot: payload_next, lambda slot: landing_next.at[slot], next_send, next_recv
     )
     each_slot(start_next)
@@ -623,20 +632,19 @@
         lanes = pl.ds(pl.multiple_of(block * WIDTH, WIDTH), WIDTH)
         for end in range(2):
             lower = dest_ref[pl.ds(end, 1), lanes] & 255
-            lowers[block, end] = jnp.where(low_ids == lower, 1.0, 0.0).astype(BF16)
+            lowers[block, :, pl.ds(end * WIDTH, WIDTH)] = jnp.where(
+                low_ids == lower, 1.0, 0.0
+            ).astype(BF16)
         return carry
 
     lax.fori_loop(0, SEG // WIDTH, fill_lowers, 0)
 
-    def take_next(slot):
-        wait_next(slot)
-        _, inside = place.beside(slot)
-
-        @pl.when(inside)
-        def _():
-            fill_places(sides, GROUPS + slot, [landing_next[slot, row] for row in range(3)])
-
-    each_slot(take_next)
+    def take_next(slot, carry):
+        fill_places(sides, GROUPS + slot, [landing_next[slot, row] for row in range(3)])
+        return carry
+
+    each_slot(wait_next)
+    lax.fori_loop(0, 27, take_next, 0)
     near_pass(
         1, live, target_ref, from_ref, target_row[...], group_row[...], sides, targets, pairs, near
     )
@@ -657,22 +665,23 @@
         def add(block, carry):
             lanes = pl.ds(pl.multiple_of(block * WIDTH, WIDTH), WIDTH)
             parts = [halves_of(values[pl.ds(row, 1), lanes]) for row in range(3)]
+            lefts = []
             for end in range(2):
                 dest = dest_ref[pl.ds(end, 1), lanes]
                 slot = dest >> 12
                 upper = jnp.where(slot == 13, 0, 16 + 4 * slot) + ((dest & (SEG - 1)) >> 8)
                 chosen = high_ids == upper
-                left = jnp.concatenate(
+                lefts.append(
                     [
                         jnp.where(chosen, parts[row][piece], 0.0).astype(BF16)
                         for row in range(3)
                         for piece in range(2)
-                    ],
-                    axis=0,
+                    ]
                 )
-                totals[...] += lax.dot_general(
-                    left, lowers[block, end], NT, preferred_element_type=F32
-                )
+            left = jnp.concatenate(
+                [jnp.concatenate(both, axis=1) for both in zip(*lefts)], axis=0
+            )
+            totals[...] += lax.dot_general(left, lowers[block], NT, preferred_element_type=F32)
             return carry
 
         lax.fori_loop(0, SEG // WIDTH, add, 0)
@@ -684,7 +693,7 @@
             both = sums[pl.ds(at, 4), :] + sums[pl.ds(at + 112, 4), :]
             leaving[slot, row, pl.ds(0, 4), :] = both[:, :TILE]
             leaving[slot, row, pl.ds(4, 4), :] = both[:, TILE:]
-    start_node, wait_node = exchange(
+    start_node, wait_node, wait_node_sent = exchange(
         place, lambda slot: leaving.at[slot], lambda slot: landed.at[slot], node_send, node_recv
     )
     each_slot(start_node)
@@ -699,7 +708,8 @@
     for row in range(3):
         total = landed[0, row]
         for slot in range(1, 27):
-            total = total + landed[slot, row]
+            if slot != 13:
+                total = total + landed[slot, row]
         for part in range(4):
             for half in range(2):
                 lanes = slice(TILE * half, TILE * half + TILE)
@@ -716,6 +726,8 @@
             copy.wait_send()
 
     each_slot(wait_ghost_send)
+    each_slot(wait_next_sent)
+    each_slot(wait_node_sent)
 
 
 def on_device(
@@ -767,7 +779,7 @@
         (3 * PAIRS, TILE),
         (3 * SEG // TILE, TILE),
         (8, SEG),
-        (SEG // WIDTH, 2, 256, WIDTH, BF16),
+        (SEG // WIDTH, 256, 2 * WIDTH, BF16),
         (96, 256),
         (672, 256),
         (27, 3, 8, TILE),

time: 70.5 us -> 64.1 us (0.909)
  Pallas kernels: 66.3 us -> 59.7 us
    pallas_call x1, Pallas kernels: 66.3 us -> 59.7 us  [on_device(): pl.pallas_call(functools.partial(step_kernel, sizes), out_shape=(shape((3...]
where the time goes in v3:
time: 64.1 us; the launch traced here: 63.8 us
  Pallas kernels  59.7 us (93%)
  local copies, waits for them, and re-layouts  2.15 us (3%)
  between operations  1.94 us (3%)
    pallas_call x1, Pallas kernels, on_device(): pl.pallas_call(functools.partial(step_kernel, sizes), out_shape=(shape((3...  59.7 us
    unnamed x4, local copies, waits for them, and re-layouts  2.15 us

profile of v3, /device:TPU:35, one launch (start us, length us, event | category | flops | bytes accessed | tf_op | source)
XLA Modules:
  0.0 63.8 jit_solution(15732045471343211838)
XLA Ops:
  1.9 59.7 %step.1 = (f32[3,4096]{1,0:T(4,128)}, f32[3,4096]{1,0:T(4,128)}) custom-call(s32[8]{0:T(128)} %ghost_ref.1, s32[1]{0:T(128)S(6)} %copy.15.live_ref, s32[1]{0:T(128)S(6)} %copy.16.count_ref, s32[128]{0:T(128)} %target_ref.1, s32[128]{0:T(128)} %from_ref.1, f32[3,4096]{1,0:T(4,128)} %rel_hbm.1, f32[3,4096]{1,0:T(4,128)} %burg_hbm.1, f32[3,4096]{1,0:T(4,128)} %line_hbm.1, ...), custom_call_target="tpu_custom_call" | custom-call | tf_op jit(solution)/shard_map/step/pallas_call | solution.py:794
  61.6 0.0 copy-start
  61.6 1.5 %copy.17 = f32[3,4096]{1,0:T(4,128)} copy(f32[3,4096]{1,0:T(4,128)} %get-tuple-element.4) | data formatting | bytes 98304
  63.1 0.0 copy-done
  63.1 0.6 copy.18
Async XLA Ops:
  61.6 1.5 %copy-start = (f32[3,4096]{1,0:T(4,128)S(1)}, f32[3,4096]{1,0:T(4,128)}, u32[]{:S(2)}) copy-start(f32[3,4096]{1,0:T(4,128)} %get-tuple-element.5) | copy-start | bytes 147460

commit v4 on v3

--- a/solution.py
+++ b/solution.py
@@ -173,7 +173,7 @@
 
 SIDE = 48 * 8
 ACROSS = 80 * 8
-UNROLL = 16
+UNROLL = 32
 WIDTH = 512
 
 
@@ -284,11 +284,11 @@
 
 def step_kernel(
     sizes,
-    ghost_ref,
-    live_ref,
-    count_ref,
-    target_ref,
-    from_ref,
+    ghost_hbm,
+    live_hbm,
+    count_hbm,
+    target_scalars,
+    from_hbm,
     rel_hbm,
     burg_hbm,
     line_hbm,
@@ -296,6 +296,13 @@
     dest_hbm,
     target_hbm,
     group_hbm,
+    moved_hbm,
+    nodes_hbm,
+    ghost_ref,
+    live_ref,
+    count_ref,
+    target_ref,
+    from_ref,
     moved_ref,
     nodes_ref,
     rel_ref,
@@ -332,6 +339,7 @@
     leaving,
     landed,
     load_sem,
+    out_sem,
     ghost_send,
     ghost_recv,
     next_send,
@@ -347,6 +355,11 @@
         pltpu.make_async_copy(source, target, load_sem.at[at])
         for at, (source, target) in enumerate(
             [
+                (ghost_hbm, ghost_ref),
+                (live_hbm, live_ref),
+                (count_hbm, count_ref),
+                (target_scalars, target_ref),
+                (from_hbm, from_ref),
                 (rel_hbm, rel_ref),
                 (burg_hbm, burg_ref),
                 (line_hbm, line_ref),
@@ -658,6 +671,9 @@
                 moved_ref[pl.ds(row, 1), lanes] = moved[tile : tile + 1]
                 values[pl.ds(row, 1), lanes] = half[tile : tile + 1]
 
+    save_moved = pltpu.make_async_copy(moved_ref, moved_hbm, out_sem.at[0])
+    save_moved.start()
+
     def scatter(first, count, totals):
         totals[...] = jnp.zeros(totals.shape, F32)
         high_ids = lax.broadcasted_iota(jnp.int32, (count, WIDTH), 0) + first
@@ -704,6 +720,11 @@
     for row in range(3):
         for part in range(4, 16):
             nodes_ref[pl.ds(row, 1), pl.ds(256 * part, 256)] = middle[row][part : part + 1]
+    inner = pl.ds(1024, SEG - 1024)
+    save_inner = pltpu.make_async_copy(
+        nodes_ref.at[:, inner], nodes_hbm.at[:, inner], out_sem.at[1]
+    )
+    save_inner.start()
     each_slot(wait_node)
     for row in range(3):
         total = landed[0, row]
@@ -718,6 +739,12 @@
                     + total[4 * half + part : 4 * half + part + 1]
                 )
 
+    outer = pl.ds(0, 1024)
+    save_outer = pltpu.make_async_copy(
+        nodes_ref.at[:, outer], nodes_hbm.at[:, outer], out_sem.at[2]
+    )
+    save_outer.start()
+
     def wait_ghost_send(slot):
         copy, inside = ghost_copy(slot)
 
@@ -728,6 +755,8 @@
     each_slot(wait_ghost_send)
     each_slot(wait_next_sent)
     each_slot(wait_node_sent)
+    for save in (save_moved, save_inner, save_outer):
+        save.wait()
 
 
 def on_device(
@@ -751,6 +780,8 @@
     dma = pltpu.SemaphoreType.DMA
     block = (GROUPS, 3, 8, TILE)
     buffers = [
+        (3, SEG),
+        (3, SEG),
         (3, SEG),
         (3, SEG),
         (3, SEG),
@@ -794,10 +825,13 @@
     return pl.pallas_call(
         functools.partial(step_kernel, sizes),
         out_shape=(shape((3, SEG), F32), shape((3, SEG), F32)),
-        in_specs=smem(5) + [pl.BlockSpec(memory_space=pl.ANY)] * 7,
-        out_specs=tuple(vmem(2)),
-        scratch_shapes=scratch
-        + [dma((7,))]
+        in_specs=[pl.BlockSpec(memory_space=pl.ANY)] * 12,
+        out_specs=(pl.BlockSpec(memory_space=pl.ANY),) * 2,
+        scratch_shapes=[
+            pltpu.SMEM((count,), jnp.int32) for count in (GHOST_DEV, 1, 1, PAIRS, PAIRS)
+        ]
+        + scratch
+        + [dma((12,)), dma((3,))]
         + [dma((27,))] * 6
         + [dma((plane,))] * 2
         + [dma((nx,))] * 2,

time: 64.1 us -> 62.4 us (0.973)
  Pallas kernels: 59.7 us -> 58.1 us
    pallas_call x1, Pallas kernels: 59.7 us -> 58.1 us  [on_device(): pl.pallas_call(functools.partial(step_kernel, sizes), out_shape=(shape((3...]
where the time goes in v4:
time: 62.4 us; the launch traced here: 62.2 us
  Pallas kernels  58.1 us (93%)
  local copies, waits for them, and re-layouts  2.15 us (3%)
  between operations  1.94 us (3%)
    pallas_call x1, Pallas kernels, on_device(): pl.pallas_call(functools.partial(step_kernel, sizes), out_shape=(shape((3...  58.1 us
    unnamed x4, local copies, waits for them, and re-layouts  2.15 us

profile of v4, /device:TPU:35, one launch (start us, length us, event | category | flops | bytes accessed | tf_op | source)
XLA Modules:
  0.0 62.2 jit_solution(15300875923745120578)
XLA Ops:
  1.9 58.1 %step.1 = (f32[3,4096]{1,0:T(4,128)}, f32[3,4096]{1,0:T(4,128)}) custom-call(s32[8]{0:T(128)} %ghost_hbm.1, s32[1]{0:T(128)S(6)} %copy.15.live_hbm, s32[1]{0:T(128)S(6)} %copy.16.count_hbm, s32[128]{0:T(128)} %target_scalars.1, s32[128]{0:T(128)} %from_hbm.1, f32[3,4096]{1,0:T(4,128)} %rel_hbm.1, f32[3,4096]{1,0:T(4,128)} %burg_hbm.1, f32[3,4096]{1,0:T(4,128)} %line_hbm.1, ...), custom_call_target="tpu_custom_call" | custom-call | tf_op jit(solution)/shard_map/step/pallas_call | solution.py:825
  60.1 0.0 copy-start
  60.1 1.5 %copy.17 = f32[3,4096]{1,0:T(4,128)} copy(f32[3,4096]{1,0:T(4,128)} %get-tuple-element.4) | data formatting | bytes 98304
  61.6 0.0 copy-done
  61.6 0.6 %copy.18 = f32[3,4096]{1,0:T(4,128)} copy(f32[3,4096]{1,0:T(4,128)S(1)} %copy-done) | data formatting | bytes 98304
Async XLA Ops:
  60.1 1.5 %copy-start = (f32[3,4096]{1,0:T(4,128)S(1)}, f32[3,4096]{1,0:T(4,128)}, u32[]{:S(2)}) copy-start(f32[3,4096]{1,0:T(4,128)} %get-tuple-element.5) | copy-start | bytes 147460

commit v5 on v4

--- a/solution.py
+++ b/solution.py
@@ -86,6 +86,13 @@
             if step:
                 inside = free[step] if inside is None else jnp.logical_and(inside, free[step])
         return where, inside
+
+    def inside(self, step_x, step_z):
+        found = True
+        for free, step in ((self.free[0], step_x), (self.free[2], step_z)):
+            if step:
+                found = free[step] if found is True else jnp.logical_and(found, free[step])
+        return found
 
     def count_beside(self):
         total = 1
@@ -489,17 +496,60 @@
             device_id_type=MESH,
         )
 
-    def ghost_copy(slot):
-        where, inside = place.beside(slot)
-        copy = pltpu.make_async_remote_copy(
-            src_ref=payload,
-            dst_ref=landing.at[26 - slot],
-            send_sem=ghost_send.at[slot],
-            recv_sem=ghost_recv.at[26 - slot],
+    toward = 1 - 2 * lax.rem(gy, 2)
+
+    def slot_of(step_x, step_y, step_z):
+        return (step_x + 1) * 9 + (step_y + 1) * 3 + step_z + 1
+
+    def ghost_copy(source, where, slot, at):
+        return pltpu.make_async_remote_copy(
+            src_ref=source,
+            dst_ref=landing.at[slot],
+            send_sem=ghost_send.at[at],
+            recv_sem=ghost_recv.at[slot],
             device_id=where,
             device_id_type=MESH,
         )
-        return copy, inside
+
+    def level_copy(step_x, step_z):
+        return ghost_copy(
+            payload,
+            (gx + step_x, gy, gz + step_z),
+            slot_of(-step_x, 0, -step_z),
+            slot_of(step_x, 0, step_z),
+        )
+
+    def partner_copy():
+        return ghost_copy(payload, (gx, gy + toward, gz), slot_of(0, -toward, 0), 13)
+
+    def away_copy(step_x, step_z):
+        return ghost_copy(
+            payload,
+            (gx + step_x, gy - toward, gz + step_z),
+            slot_of(-step_x, toward, -step_z),
+            slot_of(step_x, -1, step_z),
+        )
+
+    def handed_copy(step_x, step_z):
+        return ghost_copy(
+            landing.at[slot_of(step_x, 0, step_z)],
+            (gx, gy + toward, gz),
+            slot_of(step_x, -toward, step_z),
+            slot_of(step_x, 1, step_z),
+        )
+
+    def each_level(body, centre=False):
+        for step_x in (-1, 0, 1):
+            for step_z in (-1, 0, 1):
+                if centre or step_x or step_z:
+                    pl.when(place.inside(step_x, step_z))(
+                        functools.partial(body, step_x, step_z)
+                    )
+
+    def each_away(body):
+        @pl.when(jnp.logical_and(gy - toward >= 0, gy - toward < ny))
+        def _():
+            each_level(body, True)
 
     def start_plane(step, carry):
         plane_copy(step).start()
@@ -507,14 +557,9 @@
 
     lax.fori_loop(1, plane, start_plane, 0)
 
-    def start_ghost(slot):
-        copy, inside = ghost_copy(slot)
-
-        @pl.when(inside)
-        def _():
-            copy.start()
-
-    each_slot(start_ghost)
+    each_level(lambda x, z: level_copy(x, z).start())
+    partner_copy().start()
+    each_away(lambda x, z: away_copy(x, z).start())
 
     def clear(slot):
         _, inside = place.beside(slot)
@@ -573,13 +618,22 @@
         return carry
 
     lax.fori_loop(1, nx, start_line, 0)
-    def wait_ghost(slot):
-        copy, _ = ghost_copy(26 - slot)
-        _, inside = place.beside(slot)
-
-        @pl.when(inside)
-        def _():
-            copy.wait_recv()
+    def hand_on(step_x, step_z):
+        level_copy(-step_x, -step_z).wait_recv()
+        handed_copy(step_x, step_z).start()
+
+    def wait_handed(step_x, step_z):
+        slot = slot_of(step_x, toward, step_z)
+        ghost_copy(payload, place.at, slot, 0).wait_recv()
+
+    def wait_away(step_x, step_z):
+        slot = slot_of(step_x, -toward, step_z)
+        ghost_copy(payload, place.at, slot, 0).wait_recv()
+
+    each_level(hand_on)
+    wait_handed(0, 0)
+    each_away(wait_away)
+    each_level(wait_handed)
 
     def take_ghosts(slot, carry):
         block = [landing[slot, row] for row in range(9)]
@@ -587,7 +641,6 @@
         fill_places(sides, GROUPS + slot, block[0:3])
         return carry
 
-    each_slot(wait_ghost)
     lax.fori_loop(0, 27, take_ghosts, 0)
     live = count_ref[0]
     near_pass(
@@ -685,28 +738,31 @@
             for end in range(2):
                 dest = dest_ref[pl.ds(end, 1), lanes]
                 slot = dest >> 12
-                upper = jnp.where(slot == 13, 0, 16 + 4 * slot) + ((dest & (SEG - 1)) >> 8)
+                first_row = jnp.where(slot > 13, 12 + 4 * slot, 16 + 4 * slot)
+                upper = jnp.where(slot == 13, 0, first_row) + ((dest & (SEG - 1)) >> 8)
                 chosen = high_ids == upper
                 lefts.append(
                     [
-                        jnp.where(chosen, parts[row][piece], 0.0).astype(BF16)
+                        jnp.where(chosen, parts[row][piece], 0.0)
                         for row in range(3)
                         for piece in range(2)
                     ]
                 )
             left = jnp.concatenate(
                 [jnp.concatenate(both, axis=1) for both in zip(*lefts)], axis=0
-            )
+            ).astype(BF16)
             totals[...] += lax.dot_general(left, lowers[block], NT, preferred_element_type=F32)
             return carry
 
         lax.fori_loop(0, SEG // WIDTH, add, 0)
 
-    scatter(16, 112, sums)
+    scatter(16, 104, sums)
     for row in range(3):
         for slot in range(27):
-            at = 224 * row + 4 * slot
-            both = sums[pl.ds(at, 4), :] + sums[pl.ds(at + 112, 4), :]
+            if slot == 13:
+                continue
+            at = 208 * row + 4 * (slot - (slot > 13))
+            both = sums[pl.ds(at, 4), :] + sums[pl.ds(at + 104, 4), :]
             leaving[slot, row, pl.ds(0, 4), :] = both[:, :TILE]
             leaving[slot, row, pl.ds(4, 4), :] = both[:, TILE:]
     start_node, wait_node, wait_node_sent = exchange(
@@ -745,14 +801,10 @@
     )
     save_outer.start()
 
-    def wait_ghost_send(slot):
-        copy, inside = ghost_copy(slot)
-
-        @pl.when(inside)
-        def _():
-            copy.wait_send()
-
-    each_slot(wait_ghost_send)
+    each_level(lambda x, z: level_copy(x, z).wait_send())
+    partner_copy().wait_send()
+    each_away(lambda x, z: away_copy(x, z).wait_send())
+    each_level(lambda x, z: handed_copy(x, z).wait_send())
     each_slot(wait_next_sent)
     each_slot(wait_node_sent)
     for save in (save_moved, save_inner, save_outer):
@@ -812,7 +864,7 @@
         (8, SEG),
         (SEG // WIDTH, 256, 2 * WIDTH, BF16),
         (96, 256),
-        (672, 256),
+        (624, 256),
         (27, 3, 8, TILE),
         (27, 3, 8, TILE),
     ]

time: 62.4 us -> 58.5 us (0.938)
  the two profiles are of different devices: /device:TPU:35 before, /device:TPU:1 now
where the time goes in v5:
time: 58.5 us; the launch traced here: 58.3 us
  Pallas kernels  54.2 us (93%)
  local copies, waits for them, and re-layouts  2.15 us (4%)
  between operations  1.94 us (3%)
    pallas_call x1, Pallas kernels, on_device(): pl.pallas_call(functools.partial(step_kernel, sizes), out_shape=(shape((3...  54.2 us
    unnamed x4, local copies, waits for them, and re-layouts  2.15 us

profile of v5, /device:TPU:1, one launch (start us, length us, event | category | flops | bytes accessed | tf_op | source)
XLA Modules:
  0.0 58.3 jit_solution(10478376809377068424)
XLA Ops:
  1.9 54.2 %step.1 = (f32[3,4096]{1,0:T(4,128)}, f32[3,4096]{1,0:T(4,128)}) custom-call(s32[8]{0:T(128)} %ghost_hbm.1, s32[1]{0:T(128)S(6)} %copy.15.live_hbm, s32[1]{0:T(128)S(6)} %copy.16.count_hbm, s32[128]{0:T(128)} %target_scalars.1, s32[128]{0:T(128)} %from_hbm.1, f32[3,4096]{1,0:T(4,128)} %rel_hbm.1, f32[3,4096]{1,0:T(4,128)} %burg_hbm.1, f32[3,4096]{1,0:T(4,128)} %line_hbm.1, ...), custom_call_target="tpu_custom_call" | custom-call | tf_op jit(solution)/shard_map/step/pallas_call | solution.py:877
  56.1 0.0 copy-start
  56.1 1.5 %copy.17 = f32[3,4096]{1,0:T(4,128)} copy(f32[3,4096]{1,0:T(4,128)} %get-tuple-element.4) | data formatting | bytes 98304
  57.6 0.0 copy-done
  57.6 0.6 %copy.18 = f32[3,4096]{1,0:T(4,128)} copy(f32[3,4096]{1,0:T(4,128)S(1)} %copy-done) | data formatting | bytes 98304
Async XLA Ops:
  56.1 1.5 %copy-start = (f32[3,4096]{1,0:T(4,128)S(1)}, f32[3,4096]{1,0:T(4,128)}, u32[]{:S(2)}) copy-start(f32[3,4096]{1,0:T(4,128)} %get-tuple-element.5) | copy-start | bytes 147460

commit v6 on v5

--- a/solution.py
+++ b/solution.py
@@ -101,10 +101,15 @@
         return total - 1
 
 
+SLOTS = sorted(
+    (slot for slot in range(27) if slot != 13),
+    key=lambda slot: (slot // 9 == 1) + (slot // 3 % 3 == 1) + (slot % 3 == 1),
+)
+
+
 def each_slot(body):
-    for slot in range(27):
-        if slot != 13:
-            body(slot)
+    for slot in SLOTS:
+        body(slot)
 
 
 def greet_neighbours(place, barrier):
@@ -546,6 +551,10 @@
                         functools.partial(body, step_x, step_z)
                     )
 
+    def hand_on(step_x, step_z):
+        level_copy(-step_x, -step_z).wait_recv()
+        handed_copy(step_x, step_z).start()
+
     def each_away(body):
         @pl.when(jnp.logical_and(gy - toward >= 0, gy - toward < ny))
         def _():
@@ -598,6 +607,7 @@
         return carry
 
     lax.fori_loop(1, plane, wait_plane, 0)
+    each_level(hand_on)
     contrib[...] = jnp.dot(
         weight, gathered[...], precision=lax.Precision.HIGHEST, preferred_element_type=F32
     )
@@ -618,10 +628,6 @@
         return carry
 
     lax.fori_loop(1, nx, start_line, 0)
-    def hand_on(step_x, step_z):
-        level_copy(-step_x, -step_z).wait_recv()
-        handed_copy(step_x, step_z).start()
-
     def wait_handed(step_x, step_z):
         slot = slot_of(step_x, toward, step_z)
         ghost_copy(payload, place.at, slot, 0).wait_recv()
@@ -630,7 +636,6 @@
         slot = slot_of(step_x, -toward, step_z)
         ghost_copy(payload, place.at, slot, 0).wait_recv()
 
-    each_level(hand_on)
     wait_handed(0, 0)
     each_away(wait_away)
     each_level(wait_handed)

time: 58.5 us -> 58.2 us (level)
  the two profiles are of different devices: /device:TPU:1 before, /device:TPU:35 now
where the time goes in v6:
time: 58.2 us; the launch traced here: 58 us
  Pallas kernels  53.9 us (93%)
  local copies, waits for them, and re-layouts  2.15 us (4%)
  between operations  1.94 us (3%)
    pallas_call x1, Pallas kernels, on_device(): pl.pallas_call(functools.partial(step_kernel, sizes), out_shape=(shape((3...  53.9 us
    unnamed x4, local copies, waits for them, and re-layouts  2.15 us

profile of v6, /device:TPU:35, one launch (start us, length us, event | category | flops | bytes accessed | tf_op | source)
XLA Modules:
  0.0 58.0 jit_solution(2181644006760679309)
XLA Ops:
  1.9 53.9 %step.1 = (f32[3,4096]{1,0:T(4,128)}, f32[3,4096]{1,0:T(4,128)}) custom-call(s32[8]{0:T(128)} %ghost_hbm.1, s32[1]{0:T(128)S(6)} %copy.15.live_hbm, s32[1]{0:T(128)S(6)} %copy.16.count_hbm, s32[128]{0:T(128)} %target_scalars.1, s32[128]{0:T(128)} %from_hbm.1, f32[3,4096]{1,0:T(4,128)} %rel_hbm.1, f32[3,4096]{1,0:T(4,128)} %burg_hbm.1, f32[3,4096]{1,0:T(4,128)} %line_hbm.1, ...), custom_call_target="tpu_custom_call" | custom-call | tf_op jit(solution)/shard_map/step/pallas_call | solution.py:882
  55.9 0.0 copy-start
  55.9 1.5 %copy.17 = f32[3,4096]{1,0:T(4,128)} copy(f32[3,4096]{1,0:T(4,128)} %get-tuple-element.4) | data formatting | bytes 98304
  57.4 0.0 copy-done
  57.4 0.6 %copy.18 = f32[3,4096]{1,0:T(4,128)} copy(f32[3,4096]{1,0:T(4,128)S(1)} %copy-done) | data formatting | bytes 98304
Async XLA Ops:
  55.9 1.5 %copy-start = (f32[3,4096]{1,0:T(4,128)S(1)}, f32[3,4096]{1,0:T(4,128)}, u32[]{:S(2)}) copy-start(f32[3,4096]{1,0:T(4,128)} %get-tuple-element.5) | copy-start | bytes 147460
